TPU v7x, 32 devices: a whole 2x2x4 slice. The times are simulated.
32 devices in a mesh: tok: 16 (over z, y, core), head: 2 (over x).
Axes of the slice: x: 2, y: 2, z: 4, core: 2. Of those that a mesh axis runs over, the one named last changes fastest.
Arguments:
- hidden: bfloat16 [512, 2048], P('tok', 'head'), may hold values from -24 to 24
- attn_gain: float32 [2048], replicated, may hold values from 0.1 to 1.9
- w_query: bfloat16 [2048, 3072], P(None, 'head'), may hold values from -0.125 to 0.125
- w_latent: bfloat16 [2048, 576], P('head'), may hold values from -0.125 to 0.125
- w_key_up: bfloat16 [16, 128, 512], P('head'), may hold values from -0.5 to 0.5
- w_value_up: bfloat16 [16, 512, 128], P('head'), may hold values from -1 to 1
- w_out: bfloat16 [2048, 2048], P('head'), may hold values from -0.125 to 0.125
- latent_cache: bfloat16 [159744, 576], P(('tok', 'head')), may hold values from -6 to 6
- cache_lengths: int32 [512], P('tok'), may hold values from 144 to 2048, as said below
- request_slot: int32 [512], P('tok'), may hold values from 0 to 511, as said below
- ffn_gain: float32 [2048], P('head'), may hold values from 0.1 to 1.9
- w_router: bfloat16 [2048, 16], P('head'), may hold values from -0.25 to 0.25
- routes: int32 [512, 6], P('tok'), may hold values from 0 to 15, all different within a row; in each aligned block of 32 rows (0 to 31, 32 to 63, ...) at most 24 rows name the same one
- expert_gate: bfloat16 [16, 2048, 1408], P('tok', None, 'head'), may hold values from -0.125 to 0.125
- expert_up: bfloat16 [16, 2048, 1408], P('tok', None, 'head'), may hold values from -0.125 to 0.125
- expert_down: bfloat16 [16, 1408, 2048], P('tok', 'head'), may hold values from -0.15625 to 0.15625
Outputs:
- new_entry: bfloat16 [512, 576], P('tok')
- attended: bfloat16 [512, 2048], P('tok', 'head')
- expert_mix: bfloat16 [512, 2048], P('tok', 'head')
Inputs may be any that keep to these rules, and one draw needn't show every extreme that they name: `request_slot`: a permutation of the 512 slots; slot s lies on owner s // 32, so every owner holds 32 slots; the requests of one device name at most 2 slots of one owner, and every device reaches that bound. `cache_lengths`: the caches of an owner's slots lie end to end in slot order at the start of that owner's 9984 rows of latent_cache; they fill at most 9984 rows, and some owner fills all of them. `routes`: each row names 6 different experts; in the rows of one device no expert is named more than 24 times.
All inputs are finite; a program needn't handle non-finite values.
Results may differ from a plain program's by a relative error of at most 0.028.
Values may be sent and summed in bfloat16 or wider, within the bound.
A program may use at most 128 MiB of HBM per device.

v0:
```python
import jax
import jax.numpy as jnp
from jax import lax
from jax.sharding import PartitionSpec as P

D = 2048
NOPE = 128
ROPE = 64
LATENT = 512


NORM_EPS = 1e-06


def rotate_pairs(values, places):
    halfway = values.shape[-1] // 2
    freqs = 10000.0 ** (-jnp.arange(halfway, dtype=jnp.float32) / halfway)
    angles = places.astype(jnp.float32).reshape(places.shape + (1,) * (values.ndim - 1)) * freqs
    cosine = jnp.cos(angles)
    sine = jnp.sin(angles)
    first_half = values[..., :halfway]
    second_half = values[..., halfway:]
    return jnp.concatenate(
        [first_half * cosine - second_half * sine, first_half * sine + second_half * cosine],
        axis=-1,
    )


def owner_attend(all_heads, owner_lengths, latent_cache, head_index, factor):
    slot_rows = all_heads.shape[0]
    total_heads = all_heads.shape[1]
    probe_width = all_heads.shape[2]
    key_rows = latent_cache.shape[0]
    starts = jnp.cumsum(owner_lengths) - owner_lengths
    places = head_index * key_rows + jnp.arange(key_rows, dtype=jnp.int32)
    inside = (places[None, :] >= starts[:, None]) & (
        places[None, :] < (starts + owner_lengths)[:, None]
    )
    scores = factor * jnp.einsum(
        "qc,pc->qp",
        all_heads.reshape(slot_rows * total_heads, probe_width),
        latent_cache,
        preferred_element_type=jnp.float32,
    )
    scores = scores.reshape(slot_rows, total_heads, key_rows)
    weights = jnp.where(inside[:, None, :], jnp.exp(scores), 0.0).astype(jnp.bfloat16)
    numerator = jnp.einsum(
        "khp,pl->khl", weights, latent_cache[:, :LATENT], preferred_element_type=jnp.float32
    )
    denominator = jnp.sum(weights.astype(jnp.float32), axis=2)
    return (numerator, denominator)


def body(
    hidden,
    attn_gain,
    w_query,
    w_latent,
    w_key_up,
    w_value_up,
    w_out,
    latent_cache,
    cache_lengths,
    request_slot,
    ffn_gain,
    w_router,
    routes,
    expert_gate,
    expert_up,
    expert_down,
):
    local_rows = hidden.shape[0]
    quarter_width = hidden.shape[1]
    local_heads = w_key_up.shape[0]
    peer_count = lax.axis_size("tok")
    head_index = lax.axis_index("head")
    tok_index = lax.axis_index("tok")
    row_ids = jnp.arange(local_rows, dtype=jnp.int32)
    gathered = lax.all_gather(hidden, "head", axis=1, tiled=True)
    widened = gathered.astype(jnp.float32)
    inv_attn = lax.rsqrt(jnp.mean(widened * widened, axis=1, keepdims=True) + NORM_EPS)
    normed_attn = (widened * inv_attn * attn_gain).astype(jnp.bfloat16)
    normed_part = lax.dynamic_slice_in_dim(
        normed_attn, head_index * quarter_width, quarter_width, 1
    )
    compressed = lax.psum(
        jnp.dot(normed_part, w_latent, preferred_element_type=jnp.float32), "head"
    )
    latent_new = compressed[:, :LATENT]
    latent_new = latent_new * lax.rsqrt(
        jnp.mean(latent_new * latent_new, axis=1, keepdims=True) + NORM_EPS
    )
    new_entry = jnp.concatenate(
        [latent_new, rotate_pairs(compressed[:, LATENT:], cache_lengths)], axis=1
    ).astype(jnp.bfloat16)
    queries = jnp.dot(normed_attn, w_query, preferred_element_type=jnp.float32).astype(jnp.bfloat16)
    queries = queries.reshape(local_rows, local_heads, NOPE + ROPE)
    absorbed = jnp.einsum(
        "bhn,hnl->bhl", queries[:, :, :NOPE], w_key_up, preferred_element_type=jnp.float32
    ).astype(jnp.bfloat16)
    turned = rotate_pairs(queries[:, :, NOPE:].astype(jnp.float32), cache_lengths).astype(
        jnp.bfloat16
    )
    probes = jnp.concatenate([absorbed, turned], axis=2)
    factor = (NOPE + ROPE) ** (-0.5)
    self_score = factor * jnp.einsum(
        "bhc,bc->bh", probes, new_entry, preferred_element_type=jnp.float32
    )
    self_weight = jnp.exp(self_score).astype(jnp.bfloat16).astype(jnp.float32)
    per_owner = max(1, local_rows // peer_count)
    buffer_rows = peer_count * per_owner
    buffer_ids = jnp.arange(buffer_rows, dtype=jnp.int32)
    dest_owner = request_slot // local_rows
    earlier_same = (dest_owner[None, :] == dest_owner[:, None]) & (
        row_ids[None, :] < row_ids[:, None]
    )
    send_place = dest_owner * per_owner + jnp.sum(earlier_same.astype(jnp.int32), axis=1)
    all_probes, all_slots, all_lengths = (
        lax.all_gather(probes, "tok", axis=0, tiled=True),
        lax.all_gather(request_slot, "tok", axis=0, tiled=True),
        lax.all_gather(cache_lengths, "tok", axis=0, tiled=True),
    )
    total_rows = all_slots.shape[0]
    slot_hit = all_slots[None, :] == (tok_index * local_rows + row_ids)[:, None]
    request_at = jnp.sum(
        jnp.where(slot_hit, jnp.arange(total_rows, dtype=jnp.int32)[None, :], 0), axis=1
    )
    owner_probes = all_probes[request_at]
    owner_lengths = all_lengths[request_at]
    owned_here = (
        (all_slots // local_rows == tok_index).astype(jnp.int32).reshape(peer_count, local_rows)
    )
    prior_count = (jnp.cumsum(owned_here, axis=1) - owned_here).reshape(total_rows)
    back_index = request_at // local_rows * per_owner + prior_count[request_at]
    all_heads = lax.all_gather(owner_probes, "head", axis=1, tiled=True)
    numerator, denominator = owner_attend(
        all_heads, owner_lengths, latent_cache, head_index, factor
    )
    group_num, group_den = (
        lax.psum_scatter(numerator, "head", scatter_dimension=1, tiled=True),
        lax.psum_scatter(denominator, "head", scatter_dimension=1, tiled=True),
    )
    at_place = buffer_ids[:, None] == back_index[None, :]
    slot_of_place = jnp.sum(jnp.where(at_place, row_ids[None, :], 0), axis=1) + local_rows * (
        1 - jnp.max(at_place.astype(jnp.int32), axis=1)
    )
    padded_num = jnp.concatenate(
        [group_num, jnp.zeros((1, local_heads, LATENT), jnp.float32)], axis=0
    )
    padded_den = jnp.concatenate([group_den, jnp.zeros((1, local_heads), jnp.float32)], axis=0)
    got_num, got_den = (
        lax.all_to_all(
            padded_num[slot_of_place].reshape(peer_count, per_owner, local_heads, LATENT),
            "tok",
            split_axis=0,
            concat_axis=0,
            tiled=True,
        ),
        lax.all_to_all(
            padded_den[slot_of_place].reshape(peer_count, per_owner, local_heads),
            "tok",
            split_axis=0,
            concat_axis=0,
            tiled=True,
        ),
    )
    back_num = got_num.reshape(buffer_rows, local_heads, LATENT)
    back_den = got_den.reshape(buffer_rows, local_heads)
    total_num = back_num[send_place] + self_weight[:, :, None] * new_entry[:, None, :LATENT].astype(
        jnp.float32
    )
    total_den = back_den[send_place] + self_weight
    mixed_latent = (total_num / total_den[:, :, None]).astype(jnp.bfloat16)
    head_out = jnp.einsum(
        "bhl,hld->bhd", mixed_latent, w_value_up, preferred_element_type=jnp.float32
    ).astype(jnp.bfloat16)
    head_out = head_out.reshape(local_rows, local_heads * NOPE)
    attn_piece = lax.psum_scatter(
        jnp.dot(head_out, w_out, preferred_element_type=jnp.float32),
        "head",
        scatter_dimension=1,
        tiled=True,
    )
    attended = (hidden.astype(jnp.float32) + attn_piece).astype(jnp.bfloat16)
    attended_wide = attended.astype(jnp.float32)
    gained = (attended_wide * ffn_gain).astype(jnp.bfloat16)
    squares, logit_part = lax.psum(
        (
            jnp.sum(attended_wide * attended_wide, axis=1),
            jnp.dot(gained, w_router, preferred_element_type=jnp.float32),
        ),
        "head",
    )
    inv_ffn = lax.rsqrt(squares / D + NORM_EPS)
    logits = logit_part * inv_ffn[:, None]
    normed_ffn = (attended_wide * ffn_gain * inv_ffn[:, None]).astype(jnp.bfloat16)
    expert_count = w_router.shape[1]
    route_count = routes.shape[1]
    expert_ids = jnp.arange(expert_count, dtype=jnp.int32)
    named = routes[:, :, None] == expert_ids[None, None, :]
    picked = jnp.sum(jnp.where(named, logits[:, None, :], 0.0), axis=2)
    lifted = jnp.exp(picked)
    route_weight = lifted / jnp.sum(lifted, axis=1, keepdims=True)
    struck = jnp.max(named.astype(jnp.int32), axis=1)
    earlier_hits = jnp.cumsum(struck, axis=0) - struck
    capacity = min(local_rows, max(2, 2 * local_rows * route_count // expert_count))
    route_place = routes * capacity + jnp.take_along_axis(earlier_hits, routes, axis=1)
    slot_total = expert_count * capacity
    slot_ids = jnp.arange(slot_total, dtype=jnp.int32)
    filled = route_place[None, :, :] == slot_ids[:, None, None]
    source_token = jnp.sum(
        jnp.where(filled, row_ids[None, :, None], 0), axis=(1, 2)
    ) + local_rows * (1 - jnp.max(filled.astype(jnp.int32), axis=(1, 2)))
    full_rows = lax.all_gather(normed_ffn, "head", axis=1, tiled=True)
    padded_rows = jnp.concatenate(
        [full_rows, jnp.zeros((1, full_rows.shape[1]), jnp.bfloat16)], axis=0
    )
    arrived = lax.all_to_all(
        padded_rows[source_token].reshape(expert_count, capacity, full_rows.shape[1]),
        "tok",
        split_axis=0,
        concat_axis=0,
        tiled=True,
    )
    expert_in = arrived.reshape(peer_count * capacity, full_rows.shape[1])
    gate_value = jnp.dot(expert_in, expert_gate[0], preferred_element_type=jnp.float32)
    up_value = jnp.dot(expert_in, expert_up[0], preferred_element_type=jnp.float32)
    activity = (jax.nn.silu(gate_value) * up_value).astype(jnp.bfloat16)
    expert_share = lax.psum_scatter(
        jnp.dot(activity, expert_down[0], preferred_element_type=jnp.float32).astype(jnp.bfloat16),
        "head",
        scatter_dimension=1,
        tiled=True,
    )
    returned = lax.all_to_all(
        expert_share.reshape(peer_count, capacity, quarter_width),
        "tok",
        split_axis=0,
        concat_axis=0,
        tiled=True,
    )
    chosen_rows = returned.reshape(slot_total, quarter_width)[route_place]
    expert_mix = jnp.sum(route_weight[:, :, None] * chosen_rows.astype(jnp.float32), axis=1).astype(
        jnp.bfloat16
    )
    return (new_entry, attended, expert_mix)


def solution(mesh):
    in_specs = (
        P("tok", "head"),
        P(),
        P(None, "head"),
        P("head", None),
        P("head", None, None),
        P("head", None, None),
        P("head", None),
        P(("tok", "head"), None),
        P("tok"),
        P("tok"),
        P("head"),
        P("head", None),
        P("tok", None),
        P("tok", None, "head"),
        P("tok", None, "head"),
        P("tok", "head", None),
    )
    out_specs = (P("tok", None), P("tok", "head"), P("tok", "head"))
    return jax.shard_map(body, mesh=mesh, in_specs=in_specs, out_specs=out_specs, check_vma=False)
```

profile of v0, /device:TPU:0, one launch (start us, length us, event | category | flops | bytes accessed | tf_op | source)
XLA Modules:
  0.0 322.7 jit_solution(1513873526632792243)
XLA Ops:
  7.2 6.2 %all_gather.18 = bf16[32,2048]{1,0:T(8,128)(2,1)S(1)} all-gather(bf16[32,1024]{1,0:T(8,128)(2,1)} %param.16), channel_id=1, replica_groups=mesh['tok'=16,'head'=2] {'head'}, dimensions={1}, use_global_device_ids=true | all-gather | bytes 196608 | tf_op jit(solution)/shard_map/all_gather | solution.py:79
  13.6 0.8 fusion.29
  14.4 2.4 fusion.43
  16.8 3.9 %convolution_convert_fusion = bf16[32,1536]{1,0:T(8,128)(2,1)S(1)} fusion(bf16[32,2048]{1,0:T(8,128)(2,1)S(1)} %fusion.29, bf16[2048,1536]{1,0:T(8,128)(2,1)} %param.18), kind=kOutput, calls=%fused_computation.26 | convolution fusion | flops 201375744 | bytes 6520832 | tf_op jit(solution)/shard_map/dot_general | solution.py:96
  21.0 1.5 fusion.20
  22.5 17.1 %all-reduce.10.cloned.1.call-done = f32[32,576]{1,0:T(8,128)} async-done(((f32[32,576]{1,0:T(8,128)}), f32[32,576]{1,0:T(8,128)}) %all-reduce.10.cloned.1.call-update) | async-done | bytes 73744 | tf_op jit(solution)/shard_map/psum | solution.py:86
  39.6 1.5 multiply_cosine_fusion
  41.3 0.8 pad_maximum_fusion
  43.9 12.0 %all-reduce.6 = (s32[512]{0:T(512)S(1)}, s32[512]{0:T(512)S(1)}) all-reduce(s32[512]{0:T(512)S(1)} %dynamic-update-slice.1, s32[512]{0:T(512)S(1)} %dynamic-update-slice), channel_id=1, replica_groups=mesh['tok'=16,'head'=2] {'tok'}, use_global_device_ids=true, to_apply=%add.4 | all-reduce | flops 1024 | bytes 8192
  56.5 0.7 gather_fusion
  57.7 40.6 %all-gather.3.cloned.1.call-done = bf16[512,8,576]{2,0,1:T(8,128)(2,1)} async-done(((bf16[32,8,576]{2,0,1:T(8,128)(2,1)}), bf16[512,8,576]{2,0,1:T(8,128)(2,1)}) %all-gather.3.cloned.1.call-update) | async-done | bytes 4718608 | tf_op jit(solution)/shard_map/all_gather | solution.py:119
  98.3 7.8 %copy.57 = bf16[512,8,576]{2,1,0:T(8,128)(2,1)} copy(bf16[512,8,576]{2,0,1:T(8,128)(2,1)} %all-gather.3.cloned.1.call-done) | data formatting | bytes 9437184 | tf_op jit(solution)/shard_map/all_gather | solution.py:119
  106.2 3.1 gather_fusion.1
  109.3 10.7 %all-gather = bf16[32,16,576]{2,1,0:T(8,128)(2,1)S(1)} all-gather(bf16[32,8,576]{2,1,0:T(8,128)(2,1)S(1)} %gather_fusion.1), channel_id=2, replica_groups=mesh['tok'=16,'head'=2] {'head'}, dimensions={1}, use_global_device_ids=true | all-gather | bytes 884736 | tf_op jit(solution)/shard_map/all_gather | solution.py:135
  120.0 7.6 %convert_reduce_fusion = (f32[512]{0:T(512)S(1)}, bf16[512,4992]{1,0:T(8,128)(2,1)S(1)}) fusion(pred[32,4992]{1,0:T(8,128)(4,1)S(1)} %compare_and_fusion, bf16[512,576]{1,0:T(8,128)(2,1)S(1)} %bitcast.79, bf16[4992,576]{0,1:T(8,128)(2,1)} %param.23), kind=kOutput, calls=%fused_computation.10 | convolution fusion | flops 2957180416 | bytes 11614208 | tf_op jit(solution)/shard_map/qc,pc->qp/dot_general | solution.py:39
  127.6 3.9 %fusion = f32[32,16,512]{2,1,0:T(8,128)} fusion(bf16[32,16,4992]{2,1,0:T(8,128)(2,1)S(1)} %bitcast.78, bf16[4992,576]{0,1:T(8,128)(2,1)S(1)} %bitcast.77, pred[32,4992]{1,0:T(8,128)(4,1)S(1)} %compare_and_fusion), kind=kOutput, calls=%fused_computation.14 | convolution fusion | flops 2619801600 | bytes 11431936 | tf_op jit(solution)/shard_map/khp,pl->khl/dot_general | solution.py:47
  131.5 0.7 gather_fusion.2
  132.6 1.6 gather_fusion.9
  137.3 8.4 %all-reduce.5 = f32[32,16]{1,0:T(8,128)S(1)} all-reduce(f32[32,16]{1,0:T(8,128)S(1)} %reduce_sum.110), channel_id=4, replica_groups=mesh['tok'=16,'head'=2] {'head'}, use_global_device_ids=true, to_apply=%region_11.12.clone | all-reduce | flops 512 | bytes 4096
  145.8 1.2 gather_fusion.5
  146.9 3.5 %all-to-all-start.1 = ((f32[16,2,8]{2,1,0:T(2,128)}), f32[16,2,8]{2,1,0:T(2,128)S(1)}, u32[]{:S(2)}, u32[]{:S(2)}) async-start(f32[16,2,8]{2,1,0:T(2,128)} %bitcast.16), calls=%async_computation.2 | async-start | bytes 32768 | tf_op jit(solution)/shard_map/all_to_all | solution.py:159
  150.9 1.1 concatenate.21
  152.0 1.4 gather_fusion.3
  153.4 3.5 %all-to-all-done.1 = f32[16,2,8]{2,1,0:T(2,128)S(1)} async-done(((f32[16,2,8]{2,1,0:T(2,128)}), f32[16,2,8]{2,1,0:T(2,128)S(1)}, u32[]{:S(2)}, u32[]{:S(2)}) %all-to-all-start.1) | async-done | bytes 1056 | tf_op jit(solution)/shard_map/all_to_all | solution.py:159
  156.9 3.6 %all-to-all-start = ((f32[16,2,8,512]{3,2,1,0:T(8,128)}), f32[16,2,8,512]{3,2,1,0:T(8,128)S(1)}, u32[]{:S(2)}, u32[]{:S(2)}) async-start(f32[16,2,8,512]{3,2,1,0:T(8,128)} %bitcast.80), calls=%async_computation.1 | async-start | bytes 1048576 | tf_op jit(solution)/shard_map/all_to_all | solution.py:152
  161.2 0.8 fusion.70
  162.0 1.3 fusion.25
  163.3 0.7 gather_fusion.6
  164.1 10.8 %all-to-all-done = f32[16,2,8,512]{3,2,1,0:T(8,128)S(1)} async-done(((f32[16,2,8,512]{3,2,1,0:T(8,128)}), f32[16,2,8,512]{3,2,1,0:T(8,128)S(1)}, u32[]{:S(2)}, u32[]{:S(2)}) %all-to-all-start) | async-done | bytes 524320 | tf_op jit(solution)/shard_map/all_to_all | solution.py:152
  174.9 1.5 gather_fusion.4
  176.4 1.2 divide_convert_fusion
  177.6 1.6 fusion.21
  179.2 3.7 %fusion.38 = f32[32,2048]{1,0:T(8,128)} fusion(bf16[1024,2048]{1,0:T(8,128)(2,1)} %param.22, bf16[8,4,8,128]{3,2,1,0:T(8,128)(2,1)S(1)} %fusion.21), kind=kOutput, calls=%fused_computation.60 | convolution fusion | flops 134217728 | bytes 4521984 | tf_op jit(solution)/shard_map/dot_general | solution.py:179
  183.3 9.9 %reduce-scatter.7.cloned.1.call-done = f32[32,1024]{1,0:T(8,128)} async-done(((f32[32,2048]{1,0:T(8,128)}), f32[32,1024]{1,0:T(8,128)}) %reduce-scatter.7.cloned.1.call-update) | async-done | bytes 131088 | tf_op jit(solution)/shard_map/reduce_scatter | solution.py:178
  193.2 1.0 fusion.34
  194.4 5.0 %all-reduce.7 = (f32[32]{0:T(128)S(1)}, f32[32,16]{0,1:T(8,128)S(1)}) all-reduce(f32[32]{0:T(128)S(1)} %get-tuple-element.13, f32[32,16]{0,1:T(8,128)S(1)} %fusion.36), channel_id=1, replica_groups=mesh['tok'=16,'head'=2] {'head'}, use_global_device_ids=true, to_apply=%region_15.16 | all-reduce | flops 544 | bytes 4352 | tf_op jit(solution)/shard_map/psum | solution.py:187
  199.5 4.9 %all_gather.23 = bf16[32,2048]{1,0:T(8,128)(2,1)S(1)} all-gather(bf16[32,1024]{1,0:T(8,128)(2,1)S(1)} %fusion.33), channel_id=1, replica_groups=mesh['tok'=16,'head'=2] {'head'}, dimensions={1}, use_global_device_ids=true | all-gather | bytes 196608 | tf_op jit(solution)/shard_map/all_gather | solution.py:214
  204.5 3.1 gather_fusion.7
  207.6 42.0 %all_to_all.20 = bf16[16,24,2048]{2,1,0:T(8,128)(2,1)S(1)} all-to-all(bf16[16,24,2048]{2,1,0:T(8,128)(2,1)} %bitcast.75), channel_id=1, replica_groups=mesh['tok'=16,'head'=2] {'tok'}, dimensions={0} | all-to-all | bytes 3145728 | tf_op jit(solution)/shard_map/all_to_all | solution.py:218
  249.6 1.1 copy-done.1
  250.7 2.7 fusion.9
  253.4 6.8 %fusion.11 = bf16[384,2048]{1,0:T(8,128)(2,1)} fusion(bf16[1,704,2048]{2,1,0:T(8,128)(2,1)S(1)} %copy-done, bf16[384,2048]{1,0:T(8,128)(2,1)} %bitcast.83, bf16[1,2048,704]{1,2,0:T(8,128)(2,1)} %param.30, f32[384,704]{0,1:T(8,128)} %fusion.9), kind=kOutput, calls=%fused_computation.25 | convolution fusion | flops 2217000960 | bytes 9994240 | tf_op jit(solution)/shard_map/dot_general | solution.py:230
  260.2 25.7 %reduce-scatter.9.cloned.1.call-done = bf16[384,1024]{1,0:T(8,128)(2,1)} async-done(((bf16[384,2048]{1,0:T(8,128)(2,1)}), bf16[384,1024]{1,0:T(8,128)(2,1)}) %reduce-scatter.9.cloned.1.call-update) | async-done | bytes 786448 | tf_op jit(solution)/shard_map/reduce_scatter | solution.py:229
  285.8 5.7 %all-to-all-start.3 = ((bf16[16,24,1024]{2,1,0:T(8,128)(2,1)}), bf16[16,24,1024]{2,1,0:T(8,128)(2,1)}, u32[]{:S(2)}, u32[]{:S(2)}) async-start(bf16[16,24,1024]{2,1,0:T(8,128)(2,1)} %bitcast.85), calls=%async_computation.6 | async-start | bytes 1572864 | tf_op jit(solution)/shard_map/all_to_all | solution.py:235
  292.5 17.8 %all-to-all-done.3 = bf16[16,24,1024]{2,1,0:T(8,128)(2,1)} async-done(((bf16[16,24,1024]{2,1,0:T(8,128)(2,1)}), bf16[16,24,1024]{2,1,0:T(8,128)(2,1)}, u32[]{:S(2)}, u32[]{:S(2)}) %all-to-all-start.3) | async-done | bytes 786464 | tf_op jit(solution)/shard_map/all_to_all | solution.py:235
  310.3 2.5 gather_fusion.8
  312.8 1.1 reshape.446
  313.9 2.3 multiply_reduce_fusion
  (124 shorter events, 8.4 us)
Async XLA Ops:
  7.2 246.2 %copy-start = (bf16[1,704,2048]{2,1,0:T(8,128)(2,1)S(1)}, bf16[1,704,2048]{2,1,0:T(8,128)(2,1)}, u32[]{:S(2)}) copy-start(bf16[1,704,2048]{2,1,0:T(8,128)(2,1)} %param.31) | copy-start | bytes 8650756
  7.2 32.4 %all-reduce.10.cloned.1.call-start = ((), (), s32[]{:S(2)}) async-start(), calls=%async_computation.7 | async-start | bytes 163840 | tf_op jit(solution)/shard_map/psum | solution.py:86
  16.8 4.2 %copy-start.15 = (s32[32]{0:T(128)S(1)}, s32[32]{0:T(128)}, u32[]{:S(2)}) copy-start(s32[32]{0:T(128)} %param.24) | copy-start | bytes 388
  16.8 81.5 %all-gather.3.cloned.1.call-start = ((), (), s32[]{:S(2)}) async-start(), calls=%async_computation.8 | async-start | bytes 5570560 | tf_op jit(solution)/shard_map/all_gather | solution.py:119
  20.8 21.4 %copy-start.18 = (u32[32]{0:T(128)S(1)}, u32[32]{0:T(128)}, u32[]{:S(2)}) copy-start(u32[32]{0:T(128)} %constant.143) | copy-start | bytes 388
  20.8 22.9 %copy-start.16 = (s32[32]{0:T(128)S(1)}, s32[32]{0:T(128)}, u32[]{:S(2)}) copy-start(s32[32]{0:T(128)} %param.25) | copy-start | bytes 388
  42.1 108.8 %reduce-scatter.5.cloned.1.call-start = ((), (), s32[]{:S(2)}) async-start(), calls=%async_computation.9 | async-start | bytes 1572864 | tf_op jit(solution)/shard_map/reduce_scatter | solution.py:140
  109.3 18.3 %slice-start = ((s8[5750784]{0:T(1024)(128)(4,1)}), s8[4194304]{0:T(1024)(128)(4,1)S(1)}, s32[]{:S(2)}) async-start(s8[5750784]{0:T(1024)(128)(4,1)} %bitcast.76), calls=%async_computation.12 | async-start | bytes 8388608
  120.0 7.6 %slice-start.1 = ((s8[5750784]{0:T(1024)(128)(4,1)}), s8[1556480]{0:T(1024)(128)(4,1)S(1)}, s32[]{:S(2)}) async-start(s8[5750784]{0:T(1024)(128)(4,1)} %bitcast.76), calls=%async_computation.13 | async-start | bytes 3112960
  127.6 4.7 %copy-start.10 = (s32[32,6]{0,1:T(8,128)S(1)}, s32[32,6]{0,1:T(8,128)}, u32[]{:S(2)}) copy-start(s32[32,6]{0,1:T(8,128)} %param.28) | copy-start | bytes 2308
  132.3 1.9 copy-start.5
  132.6 2.4 copy-start.17
  132.6 17.8 %copy-start.3 = (f32[32,576]{1,0:T(8,128)S(1)}, f32[32,576]{1,0:T(8,128)}, u32[]{:S(2)}) copy-start(f32[32,576]{1,0:T(8,128)} %all-reduce.10.cloned.1.call-done) | copy-start | bytes 221188
  146.9 10.0 %all-to-all-start.1 = ((f32[16,2,8]{2,1,0:T(2,128)}), f32[16,2,8]{2,1,0:T(2,128)S(1)}, u32[]{:S(2)}, u32[]{:S(2)}) async-start(f32[16,2,8]{2,1,0:T(2,128)} %bitcast.16), calls=%async_computation.2 | async-start | bytes 32768 | tf_op jit(solution)/shard_map/all_to_all | solution.py:159
  156.9 18.0 %all-to-all-start = ((f32[16,2,8,512]{3,2,1,0:T(8,128)}), f32[16,2,8,512]{3,2,1,0:T(8,128)S(1)}, u32[]{:S(2)}, u32[]{:S(2)}) async-start(f32[16,2,8,512]{3,2,1,0:T(8,128)} %bitcast.80), calls=%async_computation.1 | async-start | bytes 1048576 | tf_op jit(solution)/shard_map/all_to_all | solution.py:152
  160.5 32.7 %reduce-scatter.7.cloned.1.call-start = ((), (), s32[]{:S(2)}) async-start(), calls=%async_computation.10 | async-start | bytes 393216 | tf_op jit(solution)/shard_map/reduce_scatter | solution.py:178
  177.6 5.4 %copy-start.6 = (s32[32,6]{1,0:T(8,128)S(1)}, s32[32,6]{1,0:T(8,128)}, u32[]{:S(2)}) copy-start(s32[32,6]{1,0:T(8,128)} %copy-done.5) | copy-start | bytes 2308
  177.6 5.4 %copy-start.9 = (s32[32,6]{1,0:T(8,128)S(1)}, s32[32,6]{1,0:T(8,128)}, u32[]{:S(2)}) copy-start(s32[32,6]{1,0:T(8,128)} %reshape.438) | copy-start | bytes 2308
  177.6 15.6 %copy-start.4 = (bf16[32,1024]{1,0:T(8,128)(2,1)S(1)}, bf16[32,1024]{1,0:T(8,128)(2,1)}, u32[]{:S(2)}) copy-start(bf16[32,1024]{1,0:T(8,128)(2,1)} %param.16) | copy-start | bytes 196612
  179.2 15.0 %copy-start.12 = (bf16[1024,16]{0,1:T(8,128)(2,1)S(1)}, bf16[1024,16]{0,1:T(8,128)(2,1)}, u32[]{:S(2)}) copy-start(bf16[1024,16]{0,1:T(8,128)(2,1)} %param.27) | copy-start | bytes 98308
  179.2 15.0 %copy-start.13 = (f32[1024]{0:T(1024)S(1)}, f32[1024]{0:T(1024)}, u32[]{:S(2)}) copy-start(f32[1024]{0:T(1024)} %param.26) | copy-start | bytes 12292
  183.0 102.9 %reduce-scatter.9.cloned.1.call-start = ((), (), s32[]{:S(2)}) async-start(), calls=%async_computation.11 | async-start | bytes 2359296 | tf_op jit(solution)/shard_map/reduce_scatter | solution.py:229
  194.3 13.4 %copy-start.2 = (bf16[32,1024]{1,0:T(8,128)(2,1)}, bf16[32,1024]{1,0:T(8,128)(2,1)S(1)}, u32[]{:S(2)}) copy-start(bf16[32,1024]{1,0:T(8,128)(2,1)S(1)} %get-tuple-element.14) | copy-start | bytes 196612
  207.6 43.1 %copy-start.14 = (bf16[1,2048,704]{1,2,0:T(8,128)(2,1)S(1)}, bf16[1,2048,704]{1,2,0:T(8,128)(2,1)}, u32[]{:S(2)}) copy-start(bf16[1,2048,704]{1,2,0:T(8,128)(2,1)} %param.29) | copy-start | bytes 8650756
  249.6 1.1 copy-start.1
  260.2 31.5 %copy-start.7 = (bf16[32,32]{1,0:T(8,128)(2,1)S(1)}, bf16[32,32]{1,0:T(8,128)(2,1)}, u32[]{:S(2)}) copy-start(bf16[32,32]{1,0:T(8,128)(2,1)} %get-tuple-element.25) | copy-start | bytes 6148
  260.2 31.5 %copy-start.8 = (bf16[32,32]{1,0:T(8,128)(2,1)S(1)}, bf16[32,32]{1,0:T(8,128)(2,1)}, u32[]{:S(2)}) copy-start(bf16[32,32]{1,0:T(8,128)(2,1)} %get-tuple-element.26) | copy-start | bytes 6148
  260.2 32.2 %copy-start.11 = (s32[32,6]{0,1:T(8,128)S(1)}, s32[32,6]{0,1:T(8,128)}, u32[]{:S(2)}) copy-start(s32[32,6]{0,1:T(8,128)} %param.28) | copy-start | bytes 2308
  285.8 24.4 %all-to-all-start.3 = ((bf16[16,24,1024]{2,1,0:T(8,128)(2,1)}), bf16[16,24,1024]{2,1,0:T(8,128)(2,1)}, u32[]{:S(2)}, u32[]{:S(2)}) async-start(bf16[16,24,1024]{2,1,0:T(8,128)(2,1)} %bitcast.85), calls=%async_computation.6 | async-start | bytes 1572864 | tf_op jit(solution)/shard_map/all_to_all | solution.py:235
Sparse Core Ops, SparseCore 0:
  16.9 22.6 all-reduce.9
  42.2 56.0 all-gather.2
  131.6 19.2 reduce-scatter.4
  183.1 10.0 reduce-scatter.6
  260.3 25.4 reduce-scatter.8
where the time goes:
time: 324 us; the launch traced here: 323 us
  waiting for transfers between devices  126 us (39%)
  blocking collectives  89.3 us (28%)
  matrix products  35.4 us (11%)
  local copies, waits for them, and re-layouts  31.3 us (10%)
  between operations  15.6 us (5%)
  starting transfers between devices  12.9 us (4%)
  other arithmetic  12.4 us (4%)
    all_to_all x1, blocking collectives, body(): lax.all_to_all(padded_rows[source_token].reshape(expert_count, capacity,...  42 us
    all_gather x1, waiting for transfers between devices, body(): lax.all_gather(probes, 'tok', axis=0, tiled=True)  40.6 us
    reduce_scatter x1, waiting for transfers between devices, body(): lax.psum_scatter(jnp.dot(activity, expert_down[0], preferred_element_type...  25.7 us
    unnamed x2, blocking collectives  20.4 us
    all_to_all x1, waiting for transfers between devices, body(): lax.all_to_all(expert_share.reshape(peer_count, capacity, quarter_width),...  17.8 us
    psum x1, waiting for transfers between devices, body(): lax.psum(jnp.dot(normed_part, w_latent, preferred_element_type=jnp.float3...  17.1 us
    all_to_all x1, waiting for transfers between devices, body(): lax.all_to_all(padded_num[slot_of_place].reshape(peer_count, per_owner, l...  10.8 us
    all_gather x1, blocking collectives, body(): all_heads = lax.all_gather(owner_probes, 'head', axis=1, tiled=True)  10.7 us
  transfers between devices with their start and end apart: 8, of which 8 were waited for; matrix products, arithmetic and copies ran while one was open for 7% of the time, Pallas kernels for 0%

commit v1 on v0

--- a/solution.py
+++ b/solution.py
@@ -1,6 +1,8 @@
 import jax
 import jax.numpy as jnp
 from jax import lax
+from jax.experimental import pallas as pl
+from jax.experimental.pallas import tpu as pltpu
 from jax.sharding import PartitionSpec as P
 
 D = 2048
@@ -246,6 +248,635 @@
     return (new_entry, attended, expert_mix)
 
 
+MESH_ID = pl.DeviceIdType.MESH
+KEY_BLOCK = 384
+WINDOW = 4
+VMEM_LIMIT = 48 * 1024 * 1024
+
+
+def meet(partners):
+    barrier = pltpu.get_barrier_semaphore()
+    for partner in partners:
+        pl.semaphore_signal(barrier, inc=1, device_id=partner, device_id_type=MESH_ID)
+    pl.semaphore_wait(barrier, len(partners))
+
+
+def in_vmem(count):
+    return [pl.BlockSpec(memory_space=pltpu.VMEM)] * count
+
+
+def swap_pair(arrays, number):
+    count = len(arrays)
+
+    def kernel(*refs):
+        ins, outs = refs[:count], refs[count : 2 * count]
+        send_sem, recv_sem = refs[2 * count :]
+        partner = (lax.axis_index("tok"), 1 - lax.axis_index("head"))
+        meet([partner])
+        copies = []
+        for i in range(count):
+            copy = pltpu.make_async_remote_copy(
+                src_ref=ins[i],
+                dst_ref=outs[i],
+                send_sem=send_sem.at[i],
+                recv_sem=recv_sem.at[i],
+                device_id=partner,
+                device_id_type=MESH_ID,
+            )
+            copy.start()
+            copies.append(copy)
+        for copy in copies:
+            copy.wait()
+
+    return pl.pallas_call(
+        kernel,
+        out_shape=[jax.ShapeDtypeStruct(a.shape, a.dtype) for a in arrays],
+        in_specs=in_vmem(count),
+        out_specs=in_vmem(count),
+        scratch_shapes=[pltpu.SemaphoreType.DMA((count,)), pltpu.SemaphoreType.DMA((count,))],
+        compiler_params=pltpu.CompilerParams(
+            collective_id=number, has_side_effects=True, vmem_limit_bytes=VMEM_LIMIT
+        ),
+        name=f"swap_pair_{number}",
+    )(*arrays)
+
+
+def to_owners(blocks, number):
+    peers = blocks.shape[0]
+
+    def kernel(src, out, send_sem, recv_sem, own_sem):
+        tok, head = lax.axis_index("tok"), lax.axis_index("head")
+        others = [
+            (lax.rem(tok + d, peers), head if e == 0 else 1 - head)
+            for d in range(peers)
+            for e in range(2)
+            if d + e > 0
+        ]
+        meet(others)
+        own = pltpu.make_async_copy(src.at[tok], out.at[head, tok], own_sem)
+        own.start()
+        sends = []
+        for i, (there, side) in enumerate(others):
+            copy = pltpu.make_async_remote_copy(
+                src_ref=src.at[there],
+                dst_ref=out.at[head, tok],
+                send_sem=send_sem.at[i],
+                recv_sem=recv_sem.at[head, tok],
+                device_id=(there, side),
+                device_id_type=MESH_ID,
+            )
+            copy.start()
+            sends.append(copy)
+        for there, side in others:
+            pltpu.make_async_remote_copy(
+                src_ref=src.at[there],
+                dst_ref=out.at[side, there],
+                send_sem=send_sem.at[0],
+                recv_sem=recv_sem.at[side, there],
+                device_id=(there, side),
+                device_id_type=MESH_ID,
+            ).wait_recv()
+        for copy in sends:
+            copy.wait_send()
+        own.wait()
+
+    return pl.pallas_call(
+        kernel,
+        out_shape=jax.ShapeDtypeStruct((2,) + blocks.shape, blocks.dtype),
+        in_specs=in_vmem(1),
+        out_specs=in_vmem(1)[0],
+        scratch_shapes=[
+            pltpu.SemaphoreType.DMA((2 * peers,)),
+            pltpu.SemaphoreType.DMA((2, peers)),
+            pltpu.SemaphoreType.DMA,
+        ],
+        compiler_params=pltpu.CompilerParams(
+            collective_id=number, has_side_effects=True, vmem_limit_bytes=VMEM_LIMIT
+        ),
+        name="to_owners",
+    )(blocks)
+
+
+def gather_rows(block, peers, number):
+    rows, width = block.shape
+    half = rows // 2
+    layers = peers // 4
+
+    def kernel(src, out, send_sem, recv_sem, own_sem):
+        tok, x = lax.axis_index("tok"), lax.axis_index("head")
+        z, y, core = tok // 4, (tok // 2) % 2, tok % 2
+
+        def place(z_, y_, core_):
+            return z_ * 4 + y_ * 2 + core_
+
+        across_x = (tok, 1 - x)
+        across_y = (place(z, 1 - y, core), x)
+        sibling = (place(z, y, 1 - core), x)
+        along_z = [(place(lax.rem(z + d, layers), y, core), x) for d in range(1, layers)]
+        meet([across_x, across_y, sibling] + along_z)
+
+        def spot(z_, y_, core_, x_, h):
+            start = pl.multiple_of(place(z_, y_, core_) * rows + h * half, half)
+            return out.at[pl.ds(start, half), pl.ds(pl.multiple_of(x_ * width, 128), width)]
+
+        def slot(z_, y_, core_, x_, h):
+            return ((place(z_, y_, core_) * 2) + x_) * 2 + h
+
+        sends = []
+
+        def push(target, z_, y_, core_, x_, h, fresh=False):
+            dst = spot(z_, y_, core_, x_, h)
+            copy = pltpu.make_async_remote_copy(
+                src_ref=src.at[pl.ds(h * half, half)] if fresh else dst,
+                dst_ref=dst,
+                send_sem=send_sem.at[len(sends)],
+                recv_sem=recv_sem.at[slot(z_, y_, core_, x_, h)],
+                device_id=target,
+                device_id_type=MESH_ID,
+            )
+            copy.start()
+            sends.append(copy)
+
+        def land(z_, y_, core_, x_, h):
+            dst = spot(z_, y_, core_, x_, h)
+            pltpu.make_async_remote_copy(
+                src_ref=dst,
+                dst_ref=dst,
+                send_sem=send_sem.at[0],
+                recv_sem=recv_sem.at[slot(z_, y_, core_, x_, h)],
+                device_id=sibling,
+                device_id_type=MESH_ID,
+            ).wait_recv()
+
+        for target in along_z[:1] + along_z[2:] + along_z[1:2]:
+            for h in range(2):
+                push(target, z, y, core, x, h, True)
+        for h in range(2):
+            push(across_x, z, y, core, x, h, True)
+            push(across_y, z, y, core, x, h, True)
+            push(sibling, z, y, core, x, h, True)
+        own = [
+            pltpu.make_async_copy(
+                src.at[pl.ds(h * half, half)], spot(z, y, core, x, h), own_sem.at[h]
+            )
+            for h in range(2)
+        ]
+        for copy in own:
+            copy.start()
+        turns = [0, 1, 3, 2][:layers]
+        for d in turns:
+            z_ = lax.rem(z + d, layers)
+            if d > 0:
+                for h in range(2):
+                    land(z_, y, core, x, h)
+                    push(across_x, z_, y, core, x, h)
+                    push(across_y, z_, y, core, x, h)
+                    push(sibling, z_, y, core, x, h)
+            land(z_, 1 - y, core, x, 0)
+            push(across_x, z_, 1 - y, core, x, 0)
+            push(sibling, z_, 1 - y, core, x, 0)
+            land(z_, y, core, 1 - x, 1)
+            push(across_y, z_, y, core, 1 - x, 1)
+            push(sibling, z_, y, core, 1 - x, 1)
+            land(z_, 1 - y, core, x, 1)
+            push(sibling, z_, 1 - y, core, x, 1)
+            land(z_, y, core, 1 - x, 0)
+            push(sibling, z_, y, core, 1 - x, 0)
+        for d in turns:
+            z_ = lax.rem(z + d, layers)
+            for h in range(2):
+                land(z_, 1 - y, core, 1 - x, h)
+                push(sibling, z_, 1 - y, core, 1 - x, h)
+        for d in turns:
+            z_ = lax.rem(z + d, layers)
+            for y_ in (y, 1 - y):
+                for x_ in (x, 1 - x):
+                    for h in range(2):
+                        land(z_, y_, 1 - core, x_, h)
+        for copy in sends:
+            copy.wait_send()
+        for copy in own:
+            copy.wait()
+
+    return pl.pallas_call(
+        kernel,
+        out_shape=jax.ShapeDtypeStruct((rows * peers, 2 * width), block.dtype),
+        in_specs=in_vmem(1),
+        out_specs=in_vmem(1)[0],
+        scratch_shapes=[
+            pltpu.SemaphoreType.DMA((128,)),
+            pltpu.SemaphoreType.DMA((4 * peers,)),
+            pltpu.SemaphoreType.DMA((2,)),
+        ],
+        compiler_params=pltpu.CompilerParams(
+            collective_id=number, has_side_effects=True, vmem_limit_bytes=VMEM_LIMIT
+        ),
+        name="gather_rows",
+    )(block)
+
+
+def scatter_sums(parts, peers, number):
+    layers = parts.shape[3]
+    half, full = parts.shape[4:]
+    width = full // 2
+
+    def kernel(src, out, got_core, kept, got_first, mid, got_second, last, got_z, sends, recvs):
+        tok, x = lax.axis_index("tok"), lax.axis_index("head")
+        z, y, core = tok // 4, (tok // 2) % 2, tok % 2
+
+        def place(z_, y_, core_):
+            return z_ * 4 + y_ * 2 + core_
+
+        across_x = (tok, 1 - x)
+        across_y = (place(z, 1 - y, core), x)
+        sibling = (place(z, y, 1 - core), x)
+        along_z = [(place(lax.rem(z + d, layers), y, core), x) for d in range(1, layers)]
+        meet([across_x, across_y, sibling] + along_z)
+
+        def copy_to(target, source, dest, index):
+            copy = pltpu.make_async_remote_copy(
+                src_ref=source,
+                dst_ref=dest,
+                send_sem=sends.at[index],
+                recv_sem=recvs.at[index],
+                device_id=target,
+                device_id_type=MESH_ID,
+            )
+            copy.start()
+            return copy
+
+        def columns(x_):
+            return pl.ds(pl.multiple_of(x_ * width, 128), width)
+
+        def total(first, second):
+            return first.astype(jnp.float32) + second.astype(jnp.float32)
+
+        cores = [[None, None], [None, None]]
+        for g in range(2):
+            for h in range(2):
+                y_ = (1 - y) if g == 0 else y
+                cores[h][g] = copy_to(
+                    sibling, src.at[h, 1 - core, y_], got_core.at[h, y_], 2 * h + g
+                )
+
+        def fold_core(h, y_):
+            @pl.loop(0, layers)
+            def _(z_):
+                kept[h, y_, z_] = total(src[h, core, y_, z_], got_core[h, y_, z_]).astype(
+                    kept.dtype
+                )
+
+        cores[1][0].wait_recv()
+        fold_core(1, 1 - y)
+        first_y = copy_to(across_y, kept.at[1, 1 - y], got_first.at[1], 4)
+        cores[0][0].wait_recv()
+        fold_core(0, 1 - y)
+        first_x = [
+            copy_to(
+                across_x,
+                kept.at[0, 1 - y, slice(None), slice(None), columns(1 - x)],
+                got_first.at[0, slice(None), slice(None), pl.ds(0, width)],
+                5,
+            )
+        ]
+        cores[0][1].wait_recv()
+        fold_core(0, y)
+        first_x.append(
+            copy_to(
+                across_x,
+                kept.at[0, y, slice(None), slice(None), columns(1 - x)],
+                got_first.at[0, slice(None), slice(None), pl.ds(width, width)],
+                6,
+            )
+        )
+        cores[1][1].wait_recv()
+        fold_core(1, y)
+
+        first_x[0].wait_recv()
+
+        @pl.loop(0, layers)
+        def _(z_):
+            mid[0, z_] = total(
+                kept[0, 1 - y, z_, :, columns(x)], got_first[0, z_, :, :width]
+            ).astype(mid.dtype)
+
+        second_y = copy_to(across_y, mid.at[0], got_second.at[0], 7)
+
+        first_y.wait_recv()
+
+        @pl.loop(0, layers)
+        def _(z_):
+            mid[1, z_] = total(
+                kept[1, y, z_, :, columns(1 - x)], got_first[1, z_, :, columns(1 - x)]
+            ).astype(mid.dtype)
+
+        second_x = copy_to(across_x, mid.at[1], got_second.at[1], 8)
+        first_x[1].wait_recv()
+
+        zs = []
+
+        def send_z(h):
+            for d in range(1, layers):
+                z_ = lax.rem(z + d, layers)
+                zs.append(
+                    copy_to(
+                        along_z[d - 1], last.at[h, z_], got_z.at[h, d - 1], 9 + h * layers + d - 1
+                    )
+                )
+
+        second_y.wait_recv()
+
+        @pl.loop(0, layers)
+        def _(z_):
+            last[0, z_] = (
+                total(kept[0, y, z_, :, columns(x)], got_first[0, z_, :, width:])
+                + got_second[0, z_].astype(jnp.float32)
+            ).astype(last.dtype)
+
+        send_z(0)
+        second_x.wait_recv()
+
+        @pl.loop(0, layers)
+        def _(z_):
+            last[1, z_] = (
+                total(kept[1, y, z_, :, columns(x)], got_first[1, z_, :, columns(x)])
+                + got_second[1, z_].astype(jnp.float32)
+            ).astype(last.dtype)
+
+        send_z(1)
+        for copy in zs:
+            copy.wait_recv()
+        for h in range(2):
+            acc = last[h, z].astype(jnp.float32)
+            for d in range(1, layers):
+                acc = acc + got_z[h, d - 1].astype(jnp.float32)
+            out[h] = acc.astype(out.dtype)
+        for copy in cores[0] + cores[1] + first_x + [first_y, second_y, second_x] + zs:
+            copy.wait_send()
+
+    kind = parts.dtype
+    return pl.pallas_call(
+        kernel,
+        out_shape=jax.ShapeDtypeStruct((2, half, width), kind),
+        in_specs=in_vmem(1),
+        out_specs=in_vmem(1)[0],
+        scratch_shapes=[
+            pltpu.VMEM((2, 2, layers, half, full), kind),
+            pltpu.VMEM((2, 2, layers, half, full), kind),
+            pltpu.VMEM((2, layers, half, full), kind),
+            pltpu.VMEM((2, layers, half, width), kind),
+            pltpu.VMEM((2, layers, half, width), kind),
+            pltpu.VMEM((2, layers, half, width), kind),
+            pltpu.VMEM((2, layers - 1, half, width), kind),
+            pltpu.SemaphoreType.DMA((9 + 2 * layers,)),
+            pltpu.SemaphoreType.DMA((9 + 2 * layers,)),
+        ],
+        compiler_params=pltpu.CompilerParams(
+            collective_id=number, has_side_effects=True, vmem_limit_bytes=VMEM_LIMIT
+        ),
+        name="scatter_sums",
+    )(parts)
+
+
+def ragged_attend(queries, cache, ids, bounds, base, factor):
+    slots, heads, width = queries.shape
+    blocks = cache.shape[0] // KEY_BLOCK
+
+    def kernel(ids_ref, bounds_ref, base_ref, q_ref, kv_ref, num_ref, den_ref):
+        j = pl.program_id(0)
+
+        @pl.when(j == 0)
+        def _():
+            num_ref[...] = jnp.zeros_like(num_ref)
+            den_ref[...] = jnp.zeros_like(den_ref)
+
+        kv = kv_ref[...]
+        who = [ids_ref[j * WINDOW + w] for w in range(WINDOW)]
+        some = jnp.concatenate([q_ref[r] for r in who], axis=0)
+        scores = factor * lax.dot_general(
+            some, kv, (((1,), (1,)), ((), ())), preferred_element_type=jnp.float32
+        )
+        places = (
+            base_ref[0]
+            + j * KEY_BLOCK
+            + lax.broadcasted_iota(jnp.int32, (heads, KEY_BLOCK), 1)
+        )
+        inside = jnp.concatenate(
+            [
+                ((places >= bounds_ref[r]) & (places < bounds_ref[slots + r])).astype(jnp.int32)
+                for r in who
+            ],
+            axis=0,
+        )
+        weights = jnp.where(inside > 0, jnp.exp(scores), 0.0).astype(jnp.bfloat16)
+        num = jnp.dot(weights, kv[:, :LATENT], preferred_element_type=jnp.float32)
+        den = jnp.sum(weights.astype(jnp.float32), axis=1, keepdims=True)
+        for w, r in enumerate(who):
+            rows = slice(w * heads, (w + 1) * heads)
+            num_ref[r] += num[rows]
+            den_ref[r] += jnp.broadcast_to(den[rows], (heads, 128))
+
+    return pl.pallas_call(
+        kernel,
+        out_shape=[
+            jax.ShapeDtypeStruct((slots, heads, LATENT), jnp.float32),
+            jax.ShapeDtypeStruct((slots, heads, 128), jnp.float32),
+        ],
+        grid_spec=pltpu.PrefetchScalarGridSpec(
+            num_scalar_prefetch=3,
+            grid=(blocks,),
+            in_specs=[
+                pl.BlockSpec((slots, heads, width), lambda j, *_: (0, 0, 0)),
+                pl.BlockSpec((KEY_BLOCK, width), lambda j, *_: (j, 0)),
+            ],
+            out_specs=[
+                pl.BlockSpec((slots, heads, LATENT), lambda j, *_: (0, 0, 0)),
+                pl.BlockSpec((slots, heads, 128), lambda j, *_: (0, 0, 0)),
+            ],
+        ),
+        compiler_params=pltpu.CompilerParams(vmem_limit_bytes=VMEM_LIMIT),
+        name="ragged_attend",
+    )(ids, bounds, base, queries, cache)
+
+
+def pick_rows(chosen, values):
+    return jnp.dot(
+        chosen.astype(jnp.bfloat16), values, preferred_element_type=jnp.float32
+    ).astype(values.dtype)
+
+
+def direct_body(
+    hidden,
+    attn_gain,
+    w_query,
+    w_latent,
+    w_key_up,
+    w_value_up,
+    w_out,
+    latent_cache,
+    cache_lengths,
+    request_slot,
+    ffn_gain,
+    w_router,
+    routes,
+    expert_gate,
+    expert_up,
+    expert_down,
+):
+    f32, bf16 = jnp.float32, jnp.bfloat16
+    rows, part = hidden.shape
+    peers = lax.axis_size("tok")
+    each = rows // peers
+    local_heads = w_key_up.shape[0]
+    expert_count = w_router.shape[1]
+    head = lax.axis_index("head")
+    tok = lax.axis_index("tok")
+    ids = jnp.arange(rows, dtype=jnp.int32)
+
+    owner = request_slot // rows
+    earlier = (owner[None, :] == owner[:, None]) & (ids[None, :] < ids[:, None])
+    send_place = owner * each + jnp.sum(earlier.astype(jnp.int32), axis=1)
+    placed = ids[:, None] == send_place[None, :]
+    route_mask = jnp.max(
+        (routes[:, :, None] == jnp.arange(expert_count, dtype=jnp.int32)).astype(jnp.int32), axis=1
+    )
+    meta = jnp.concatenate(
+        [
+            (request_slot % rows)[:, None],
+            (cache_lengths // 64)[:, None],
+            (cache_lengths % 64)[:, None],
+            route_mask,
+        ],
+        axis=1,
+    ).astype(bf16)
+    meta = jnp.pad(meta, ((0, 0), (0, part - meta.shape[1])))
+    sent = pick_rows(placed, jnp.concatenate([hidden, meta], axis=1))
+    blocks = sent.reshape(peers, each, 2, part).transpose(0, 2, 1, 3)
+    blocks = blocks.reshape(peers, 2 * each * part // 128, 128)
+    arrived = to_owners(blocks, 0).reshape(2, peers, 2, each, part)
+    wide = arrived[:, :, 0].reshape(2, rows, part)
+    meta = arrived[0, :, 1].reshape(rows, part)[:, : 3 + expert_count].astype(jnp.int32)
+    slot, lengths = meta[:, 0], meta[:, 1] * 64 + meta[:, 2]
+    mask = meta[:, 3:]
+    starts = jnp.sum(jnp.where(slot[None, :] < slot[:, None], lengths[None, :], 0), axis=1)
+    full = jnp.concatenate([wide[0], wide[1]], axis=1).astype(f32)
+    mine = lax.dynamic_index_in_dim(wide, head, 0, keepdims=False)
+
+    inv_attn = lax.rsqrt(jnp.mean(full * full, axis=1, keepdims=True) + NORM_EPS)
+    normed = (full * inv_attn * attn_gain).astype(bf16)
+    normed_part = lax.dynamic_slice_in_dim(normed, head * part, part, 1)
+    compressed = jnp.dot(normed_part, w_latent, preferred_element_type=f32)
+    queries = jnp.dot(normed, w_query, preferred_element_type=f32).astype(bf16)
+    queries = queries.reshape(rows, local_heads, NOPE + ROPE)
+    absorbed = jnp.einsum(
+        "bhn,hnl->bhl", queries[:, :, :NOPE], w_key_up, preferred_element_type=f32
+    ).astype(bf16)
+    turned = rotate_pairs(queries[:, :, NOPE:].astype(f32), lengths).astype(bf16)
+    probes = jnp.concatenate([absorbed, turned], axis=2)
+    far_probes, far_compressed = swap_pair([probes, compressed], 1)
+    compressed = compressed + far_compressed
+    latent_new = compressed[:, :LATENT]
+    latent_new = latent_new * lax.rsqrt(
+        jnp.mean(latent_new * latent_new, axis=1, keepdims=True) + NORM_EPS
+    )
+    new_entry = jnp.concatenate(
+        [latent_new, rotate_pairs(compressed[:, LATENT:], lengths)], axis=1
+    ).astype(bf16)
+    factor = (NOPE + ROPE) ** (-0.5)
+    self_score = factor * jnp.einsum(
+        "bhc,bc->bh", probes, new_entry, preferred_element_type=f32
+    )
+    self_weight = jnp.exp(self_score).astype(bf16).astype(f32)
+
+    key_rows = latent_cache.shape[0]
+    block_starts = head * key_rows + jnp.arange(0, key_rows, KEY_BLOCK, dtype=jnp.int32)
+    ends = starts + lengths
+    first = jnp.sum((ends[None, :] <= block_starts[:, None]).astype(jnp.int32), axis=1)
+    first = jnp.minimum(first, rows - WINDOW)
+    window = first[:, None] + jnp.arange(WINDOW, dtype=jnp.int32)
+    window_ids = jnp.sum(
+        jnp.where(window[:, :, None] == slot[None, None, :], ids[None, None, :], 0), axis=2
+    )
+    numerator, denominator = ragged_attend(
+        jnp.concatenate([probes, far_probes], axis=1),
+        latent_cache,
+        window_ids.reshape(-1).astype(jnp.int32),
+        jnp.concatenate([starts, ends]).astype(jnp.int32),
+        (head * key_rows).reshape(1).astype(jnp.int32),
+        factor,
+    )
+    denominator = denominator[:, :, 0]
+    far_num, far_den = swap_pair(
+        [
+            numerator[:, local_heads:].astype(bf16).reshape(rows * local_heads, LATENT),
+            denominator[:, local_heads:].reshape(rows * local_heads // 128, 128),
+        ],
+        2,
+    )
+    total_num = (
+        numerator[:, :local_heads]
+        + far_num.reshape(rows, local_heads, LATENT).astype(f32)
+        + self_weight[:, :, None] * new_entry[:, None, :LATENT].astype(f32)
+    )
+    total_den = denominator[:, :local_heads] + far_den.reshape(rows, local_heads) + self_weight
+    mixed = (total_num / total_den[:, :, None]).astype(bf16)
+    head_out = jnp.einsum("bhl,hld->bhd", mixed, w_value_up, preferred_element_type=f32)
+    head_out = head_out.astype(bf16).reshape(rows, local_heads * NOPE)
+    piece = jnp.dot(head_out, w_out, preferred_element_type=f32)
+    kept = lax.dynamic_slice_in_dim(piece, head * part, part, 1)
+    given = lax.dynamic_slice_in_dim(piece, (1 - head) * part, part, 1)
+    (far_piece,) = swap_pair([given], 3)
+    attended = (mine.astype(f32) + (kept + far_piece)).astype(bf16)
+
+    attended_wide = attended.astype(f32)
+    gained = (attended_wide * ffn_gain).astype(bf16)
+    squares = jnp.sum(attended_wide * attended_wide, axis=1, keepdims=True)
+    logit_part = jnp.dot(gained, w_router, preferred_element_type=f32)
+    notes = jnp.concatenate([squares, logit_part], axis=1)
+    high = notes.astype(bf16)
+    low = (notes - high.astype(f32)).astype(bf16)
+    notes = jnp.concatenate([high, low, mask.astype(bf16)], axis=1)
+    notes = jnp.pad(notes, ((0, 0), (0, 128 - notes.shape[1])))
+    gathered = gather_rows(jnp.concatenate([gained, notes], axis=1), peers, 4)
+
+    back = jnp.concatenate([attended, new_entry], axis=1).reshape(peers, each, -1)
+    back = lax.all_to_all(back, "tok", split_axis=0, concat_axis=0, tiled=True)
+    back = pick_rows(placed.T, back.reshape(rows, -1))
+
+    span = part + 128
+    tokens = jnp.concatenate([gathered[:, :part], gathered[:, span : span + part]], axis=1)
+    marks = gathered[:, part:span].astype(f32), gathered[:, span + part :].astype(f32)
+    count = 1 + expert_count
+    sums = sum(m[:, :count] + m[:, count : 2 * count] for m in marks)
+    inv_ffn = lax.rsqrt(sums[:, :1] / (2 * part) + NORM_EPS)
+    lifted = jnp.exp(sums[:, 1:] * inv_ffn) * marks[0][:, 2 * count : 2 * count + expert_count]
+    here = (jnp.arange(expert_count, dtype=jnp.int32) == tok).astype(f32)
+    weight = jnp.sum(lifted * here, axis=1) / jnp.sum(lifted, axis=1)
+    gate_value = jnp.dot(tokens, expert_gate[0], preferred_element_type=f32) * inv_ffn
+    up_value = jnp.dot(tokens, expert_up[0], preferred_element_type=f32) * inv_ffn
+    activity = (jax.nn.silu(gate_value) * up_value).astype(bf16)
+    every = jnp.arange(rows * peers, dtype=jnp.int32)
+    half = rows // 2
+    layers = peers // 4
+    h_, c_, y_, z_ = (
+        every // (half * peers),
+        every // (half * peers // 2) % 2,
+        every // (half * layers) % 2,
+        every // half % layers,
+    )
+    device = z_ * 4 + y_ * 2 + c_
+    inner = h_ * half + every % half
+    source = inner // each * rows + device * each + inner % each
+    moved = source[:, None] == every[None, :]
+    activity = pick_rows(moved, activity)
+    weight = jnp.sum(jnp.where(moved, weight[None, :], 0.0), axis=1)
+    terms = jnp.dot(activity, expert_down[0], preferred_element_type=f32) * weight[:, None]
+    terms = terms.astype(bf16).reshape(2, 2, 2, layers, half, 2 * part)
+    summed = scatter_sums(terms, peers, 5).reshape(rows, part)
+    expert_mix = pick_rows(placed.T, summed)
+    return (back[:, part:], back[:, :part], expert_mix)
+
+
 def solution(mesh):
     in_specs = (
         P("tok", "head"),
@@ -266,4 +897,5 @@
         P("tok", "head", None),
     )
     out_specs = (P("tok", None), P("tok", "head"), P("tok", "head"))
-    return jax.shard_map(body, mesh=mesh, in_specs=in_specs, out_specs=out_specs, check_vma=False)
+    chosen = direct_body if (mesh.shape["tok"], mesh.shape["head"]) == (16, 2) else body
+    return jax.shard_map(chosen, mesh=mesh, in_specs=in_specs, out_specs=out_specs, check_vma=False)

time: 324 us -> 167 us (0.52)
  waiting for transfers between devices: 126 us -> 0.01 us
  Pallas kernels: 0 us -> 97.3 us
  blocking collectives: 89.3 us -> 0 us
  between operations: 15.6 us -> 1.2 us
  local copies, waits for them, and re-layouts: 31.3 us -> 21.2 us
  starting transfers between devices: 12.9 us -> 6.45 us
  matrix products: 35.4 us -> 29.1 us
    pallas_call x0 -> x7, Pallas kernels: none -> 97.3 us  [the longest x1 25.9 us: gather_rows(): pl.pallas_call(kernel, out_shape=jax.ShapeDtypeStruct((rows * peers, 2 *...]
    all_to_all x1 -> x0, blocking collectives: 42 us -> none  [body(): lax.all_to_all(padded_rows[source_token].reshape(expert_count, capacity,...]
    all_gather x1 -> x0, waiting for transfers between devices: 40.6 us -> none  [body(): lax.all_gather(probes, 'tok', axis=0, tiled=True)]
    reduce_scatter x3 -> x0, waiting for transfers between devices: 35.9 us -> none  [the longest x1 25.7 us: body(): lax.psum_scatter(jnp.dot(activity, expert_down[0], preferred_element_type...]
    all_to_all x3 -> x1, waiting for transfers between devices: 32.1 us -> 0.01 us  [direct_body(): back = lax.all_to_all(back, 'tok', split_axis=0, concat_axis=0, tiled=True)]
    all_gather x3 -> x0, blocking collectives: 21.8 us -> none  [the longest x1 10.7 us: body(): all_heads = lax.all_gather(owner_probes, 'head', axis=1, tiled=True)]
    unnamed x2 -> x0, blocking collectives: 20.4 us -> none
    gather x12 -> x0, local copies, waits for them, and re-layouts: 17.4 us -> none  [the longest x1 3.13 us: body(): padded_rows[source_token]]
  transfers between devices with their start and end apart: 8 -> 1, of which waited for: 8 -> 0; matrix products, arithmetic and copies ran while one was open for 7% -> 11% of each run, Pallas kernels for 0% -> 29%
where the time goes in v1:
time: 167 us; the launch traced here: 166 us
  Pallas kernels  97.3 us (58%)
  matrix products  29.1 us (17%)
  local copies, waits for them, and re-layouts  21.2 us (13%)
  other arithmetic  10.5 us (6%)
  starting transfers between devices  6.45 us (4%)
    pallas_call x1, Pallas kernels, gather_rows(): pl.pallas_call(kernel, out_shape=jax.ShapeDtypeStruct((rows * peers, 2 *...  25.9 us
    pallas_call x3, Pallas kernels, swap_pair(): pl.pallas_call(kernel, out_shape=[jax.ShapeDtypeStruct(a.shape, a.dtype)...  24.5 us
    pallas_call x1, Pallas kernels, scatter_sums(): pl.pallas_call(kernel, out_shape=jax.ShapeDtypeStruct((2, half, width), k...  22.7 us
    pallas_call x1, Pallas kernels, to_owners(): pl.pallas_call(kernel, out_shape=jax.ShapeDtypeStruct((2,) + blocks.shape...  12.7 us
    unnamed x43, local copies, waits for them, and re-layouts  11.6 us
    pallas_call x1, Pallas kernels, ragged_attend(): pl.pallas_call(kernel, out_shape=[jax.ShapeDtypeStruct((slots, heads, LAT...  11.5 us
    dot_general x4, matrix products, pick_rows(): jnp.dot(chosen.astype(jnp.bfloat16), values, preferred_element_type=jnp.f...  7.99 us
    all_to_all x1, starting transfers between devices, direct_body(): back = lax.all_to_all(back, 'tok', split_axis=0, concat_axis=0, tiled=True)  6.45 us
  transfers between devices with their start and end apart: 1, of which 0 were waited for; matrix products, arithmetic and copies ran while one was open for 11% of the time, Pallas kernels for 29%

profile of v1, /device:TPU:0, one launch (start us, length us, event | category | flops | bytes accessed | tf_op | source)
XLA Modules:
  0.0 165.7 jit_solution(16656950544188995262)
XLA Ops:
  0.7 0.8 convert_bitcast_fusion
  1.5 0.7 and_select_fusion.3
  2.2 0.2 convert_reduce_fusion.2
  2.4 0.7 convert_reduce_fusion
  3.2 1.0 convolution_convert_fusion.2
  4.5 12.7 %to_owners.1 = bf16[2,16,32,128]{3,2,1,0:T(8,128)(2,1)S(1)} custom-call(bf16[16,32,128]{2,1,0:T(8,128)(2,1)S(1)} %reshape.343.src), custom_call_target="tpu_custom_call" | custom-call | tf_op jit(solution)/shard_map/to_owners/pallas_call | solution.py:343
  17.6 0.7 convert_reduce_fusion.1
  18.8 3.9 %convolution_convert_fusion = bf16[32,1536]{1,0:T(8,128)(2,1)S(1)} fusion(bf16[32,2048]{1,0:T(8,128)(2,1)S(1)} %fusion.28, bf16[2048,1536]{1,0:T(8,128)(2,1)} %param.18), kind=kOutput, calls=%fused_computation.6 | convolution fusion | flops 201375744 | bytes 6520832 | tf_op jit(solution)/shard_map/dot_general | solution.py:769
  22.9 0.7 reshape_squeeze.6
  23.9 0.2 convert_reduce_fusion.3
  24.2 0.4 select_reduce_fusion.1
  24.7 1.5 fusion.52
  26.5 1.7 %fusion.54.refs_1_ = f32[32,576]{1,0:T(8,128)S(1)} fusion(bf16[1024,576]{0,1:T(8,128)(2,1)} %param.19, bf16[32,2048]{1,0:T(8,128)(2,1)S(1)} %fusion.28, s32[]{:T(128)S(6)} %select_n.148), kind=kOutput, calls=%fused_computation.82 | convolution fusion | flops 37748736 | bytes 1318916 | tf_op jit(solution)/shard_map/dot_general | solution.py:768
  28.4 11.7 %swap_pair_1.1 = (bf16[32,8,576]{2,1,0:T(8,128)(2,1)S(1)}, f32[32,576]{1,0:T(8,128)S(1)}) custom-call(bf16[32,8,576]{2,1,0:T(8,128)(2,1)S(1)} %pad_maximum_fusion.6.refs_0_, f32[32,576]{1,0:T(8,128)S(1)} %fusion.54.refs_1_), custom_call_target="tpu_custom_call" | custom-call | tf_op jit(solution)/shard_map/swap_pair_1/pallas_call | solution.py:291
  40.2 1.1 pad_maximum_fusion.5.q_ref
  41.5 0.7 fusion.120
  42.2 0.6 copy-done.8
  42.9 0.9 fusion.46
  43.9 1.4 copy.84
  45.2 8.6 %copy.73.kv_ref = bf16[4992,576]{1,0:T(8,128)(2,1)} copy(bf16[4992,576]{0,1:T(8,128)(2,1)} %param.23) | data formatting | bytes 11501568 | tf_op args[7]
  53.8 11.5 %ragged_attend.1 = (f32[32,16,512]{2,1,0:T(8,128)S(1)}, f32[32,16,128]{2,1,0:T(8,128)S(1)}) custom-call(s32[52]{0:T(128)S(1)} %reshape.345.ids_ref, s32[64]{0:T(128)S(1)} %pad_add_fusion.bounds_ref, s32[1]{0:T(128)} %bitcast.5.base_ref, bf16[32,16,576]{2,1,0:T(8,128)(2,1)S(1)} %pad_maximum_fusion.5.q_ref, bf16[4992,576]{1,0:T(8,128)(2,1)} %copy.73.kv_ref), custom_call_target="tpu_custom_call" | custom-call | tf_op jit(solution)/shard_map/ragged_attend/pallas_call | solution.py:679
  65.3 1.0 copy-done.1
  66.3 0.7 copy-done.2
  67.0 1.1 copy.74
  68.3 1.1 fusion.30.refs_0_
  69.4 7.8 %swap_pair_2.1 = (bf16[256,512]{1,0:T(8,128)(2,1)S(1)}, f32[2,128]{1,0:T(2,128)S(1)}) custom-call(bf16[256,512]{1,0:T(8,128)(2,1)S(1)} %fusion.30.refs_0_, f32[2,128]{1,0:T(2,128)S(1)} %reshape.349.refs_1_), custom_call_target="tpu_custom_call" | custom-call | tf_op jit(solution)/shard_map/swap_pair_2/pallas_call | solution.py:291
  77.3 0.7 fusion.95
  78.2 1.2 fusion.24
  79.4 1.5 fusion.19
  81.0 3.1 %fusion.48 = f32[32,2048]{1,0:T(8,128)S(1)} fusion(bf16[1024,2048]{1,0:T(8,128)(2,1)} %param.22, bf16[8,4,8,128]{3,2,1,0:T(8,128)(2,1)S(1)} %fusion.19), kind=kOutput, calls=%fused_computation.72 | convolution fusion | flops 134217728 | bytes 4521984 | tf_op jit(solution)/shard_map/dot_general | solution.py:825
  84.1 5.0 %swap_pair_3.1 = f32[32,1024]{1,0:T(8,128)S(1)} custom-call(f32[32,1024]{1,0:T(8,128)S(1)} %constant_dynamic-slice_fusion.refs_0_), custom_call_target="tpu_custom_call" | custom-call | tf_op jit(solution)/shard_map/swap_pair_3/pallas_call | solution.py:291
  89.4 0.7 reshape.352
  90.0 6.5 %all-to-all-start = ((bf16[16,2,1600]{2,1,0:T(2,128)(2,1)}), bf16[16,2,1600]{2,1,0:T(2,128)(2,1)S(1)}, u32[]{:S(2)}, u32[]{:S(2)}) async-start(bf16[16,2,1600]{2,1,0:T(2,128)(2,1)} %reshape.352), calls=%async_computation | async-start | bytes 212992 | tf_op jit(solution)/shard_map/all_to_all | solution.py:843
  96.7 0.9 fusion.124
  97.9 25.9 %gather_rows.1 = bf16[512,2304]{1,0:T(8,128)(2,1)S(1)} custom-call(bf16[32,1152]{1,0:T(8,128)(2,1)S(1)} %pad_maximum_fusion.8.src), custom_call_target="tpu_custom_call" | custom-call | tf_op jit(solution)/shard_map/gather_rows/pallas_call | solution.py:461
  123.8 1.6 fusion.121
  125.5 0.2 fusion.35
  125.8 0.4 fusion.118
  126.3 0.3 select_reduce_fusion
  126.7 0.3 copy-done.5
  127.0 4.6 %fusion.5 = f32[512,704]{0,1:T(8,128)} fusion(bf16[1,2048,704]{1,2,0:T(8,128)(2,1)} %param.29, bf16[512,1024]{1,0:T(8,128)(2,1)S(1)} %copy-done.5, bf16[512,1024]{1,0:T(8,128)(2,1)S(1)} %copy-done.4, f32[512]{0:T(512)S(1)} %fusion.34), kind=kOutput, calls=%fused_computation.10 | convolution fusion | flops 1480949760 | bytes 6424576 | tf_op jit(solution)/shard_map/dot_general | solution.py:855
  131.6 5.9 %convolution_convert_fusion.3 = bf16[512,704]{0,1:T(8,128)(2,1)} fusion(bf16[1,2048,704]{1,2,0:T(8,128)(2,1)} %param.30, f32[512,704]{0,1:T(8,128)} %fusion.5, bf16[512,1024]{1,0:T(8,128)(2,1)} %get-tuple-element.26, bf16[512,1024]{1,0:T(8,128)(2,1)} %get-tuple-element.25, f32[512]{0:T(512)S(1)} %fusion.34, s32[512]{0:T(512)S(1)} %fusion.86), kind=kOutput, calls=%fused_computation.14 | convolution fusion | flops 1852833792 | bytes 7147520 | tf_op jit(solution)/shard_map/dot_general | solution.py:703
  137.6 2.9 %multiply_convert_fusion = bf16[512,2048]{1,0:T(8,128)(2,1)S(1)} fusion(bf16[512,704]{0,1:T(8,128)(2,1)} %convolution_convert_fusion.3, bf16[1,704,2048]{2,1,0:T(8,128)(2,1)S(1)} %copy-done, f32[512]{0:T(512)S(1)} %select_reduce_fusion), kind=kOutput, calls=%fused_computation | convolution fusion | flops 1478492160 | bytes 5703680 | tf_op jit(solution)/shard_map/dot_general | solution.py:873
  140.5 22.7 %scatter_sums.1 = bf16[2,16,1024]{2,1,0:T(8,128)(2,1)S(1)} custom-call(bf16[2,2,2,4,16,2048]{5,4,3,2,1,0:T(8,128)(2,1)S(1)} %bitcast.86), custom_call_target="tpu_custom_call" | custom-call | tf_op jit(solution)/shard_map/scatter_sums/pallas_call | solution.py:618
  163.3 0.8 convolution_convert_fusion.5
  164.2 0.2 convolution_convert_fusion.1
  164.4 0.6 slice.167
  165.0 0.6 slice.168
  (98 shorter events, 4.4 us)
Async XLA Ops:
  0.6 136.9 %copy-start = (bf16[1,704,2048]{2,1,0:T(8,128)(2,1)S(1)}, bf16[1,704,2048]{2,1,0:T(8,128)(2,1)}, u32[]{:S(2)}) copy-start(bf16[1,704,2048]{2,1,0:T(8,128)(2,1)} %param.31) | copy-start | bytes 8650756
  0.6 18.0 %copy-start.13 = (f32[2048]{0:T(1024)S(1)}, f32[2048]{0:T(1024)}, u32[]{:S(2)}) copy-start(f32[2048]{0:T(1024)} %param.17) | copy-start | bytes 24580
  0.7 25.6 %copy-start.17 = (f32[32]{0:T(128)}, f32[32]{0:T(128)S(1)}, u32[]{:S(2)}) copy-start(f32[32]{0:T(128)S(1)} %multiply_power_fusion) | copy-start | bytes 388
  2.4 0.8 copy-start.15
  17.6 0.7 copy-start.6
  26.3 13.9 %copy-start.3 = (bf16[8,32,512]{2,0,1:T(8,128)(2,1)}, bf16[8,32,512]{2,0,1:T(8,128)(2,1)S(1)}, u32[]{:S(2)}) copy-start(bf16[8,32,512]{2,0,1:T(8,128)(2,1)S(1)} %copy.104) | copy-start | bytes 786436
  26.5 14.9 %copy-start.18 = (f32[32]{0:T(128)S(1)}, f32[32]{0:T(128)}, u32[]{:S(2)}) copy-start(f32[32]{0:T(128)} %copy-done.17) | copy-start | bytes 388
  26.5 14.9 %copy-start.19 = (f32[32]{0:T(128)S(1)}, f32[32]{0:T(128)}, u32[]{:S(2)}) copy-start(f32[32]{0:T(128)} %convert_reduce_fusion.1) | copy-start | bytes 388
  41.5 1.4 copy-start.11
  42.2 0.6 copy-start.8
  65.3 1.0 copy-start.1
  66.3 0.7 copy-start.2
  80.9 8.2 %copy-start.10 = (bf16[2,32,1024]{2,1,0:T(8,128)(2,1)S(1)}, bf16[2,32,1024]{2,1,0:T(8,128)(2,1)}, u32[]{:S(2)}) copy-start(bf16[2,32,1024]{2,1,0:T(8,128)(2,1)} %reshape_squeeze.6) | copy-start | bytes 393220
  80.9 8.3 %copy-start.9 = (bf16[32,512]{1,0:T(8,128)(2,1)S(1)}, bf16[32,512]{1,0:T(8,128)(2,1)}, u32[]{:S(2)}) copy-start(bf16[32,512]{1,0:T(8,128)(2,1)} %copy-done.8) | copy-start | bytes 98308
  80.9 8.3 %copy-start.12 = (bf16[32,32]{1,0:T(8,128)(2,1)S(1)}, bf16[32,32]{1,0:T(8,128)(2,1)}, u32[]{:S(2)}) copy-start(bf16[32,32]{1,0:T(8,128)(2,1)} %copy-done.11) | copy-start | bytes 6148
  80.9 15.6 %copy-start.7 = (s32[32,19]{1,0:T(8,128)S(1)}, s32[32,19]{1,0:T(8,128)}, u32[]{:S(2)}) copy-start(s32[32,19]{1,0:T(8,128)} %copy-done.6) | copy-start | bytes 7300
  81.0 15.7 %copy-start.14 = (f32[1024]{0:T(1024)S(1)}, f32[1024]{0:T(1024)}, u32[]{:S(2)}) copy-start(f32[1024]{0:T(1024)} %param.26) | copy-start | bytes 12292
  90.0 74.1 %all-to-all-start = ((bf16[16,2,1600]{2,1,0:T(2,128)(2,1)}), bf16[16,2,1600]{2,1,0:T(2,128)(2,1)S(1)}, u32[]{:S(2)}, u32[]{:S(2)}) async-start(bf16[16,2,1600]{2,1,0:T(2,128)(2,1)} %reshape.352), calls=%async_computation | async-start | bytes 212992 | tf_op jit(solution)/shard_map/all_to_all | solution.py:843
  125.4 1.2 copy-start.4
  125.5 1.5 copy-start.5
  140.5 22.8 %copy-start.16 = (s32[32]{0:T(128)S(1)}, s32[32]{0:T(128)}, u32[]{:S(2)}) copy-start(s32[32]{0:T(128)} %copy-done.15) | copy-start | bytes 388

commit v2 on v1

--- a/solution.py
+++ b/solution.py
@@ -249,7 +249,8 @@
 
 
 MESH_ID = pl.DeviceIdType.MESH
-KEY_BLOCK = 384
+KEY_BLOCK = 1664
+KEY_CUTS = (0, 384, 768, 1152, 1536, 1664)
 WINDOW = 4
 VMEM_LIMIT = 48 * 1024 * 1024
 
@@ -301,60 +302,98 @@
     )(*arrays)
 
 
-def to_owners(blocks, number):
+def to_owners(blocks, notes, number):
     peers = blocks.shape[0]
 
-    def kernel(src, out, send_sem, recv_sem, own_sem):
+    def kernel(src, src_notes, out, out_notes, send_sem, recv_sem, pass_sem, note_sem, own_sem):
         tok, head = lax.axis_index("tok"), lax.axis_index("head")
-        others = [
-            (lax.rem(tok + d, peers), head if e == 0 else 1 - head)
-            for d in range(peers)
-            for e in range(2)
-            if d + e > 0
+        partner = (tok, 1 - head)
+        others = [lax.rem(tok + d, peers) for d in range(1, peers)]
+        meet([partner] + [(there, head) for there in others])
+
+        def remote(source, dest, first, second, target):
+            return pltpu.make_async_remote_copy(
+                src_ref=source,
+                dst_ref=dest,
+                send_sem=first,
+                recv_sem=second,
+                device_id=target,
+                device_id_type=MESH_ID,
+            )
+
+        sends = []
+        for i, there in enumerate(others):
+            sends.append(
+                remote(
+                    src.at[there],
+                    out.at[head, tok],
+                    send_sem.at[i],
+                    recv_sem.at[head, tok],
+                    (there, head),
+                )
+            )
+            sends[-1].start()
+        sends.append(
+            remote(
+                src.at[tok], out.at[head, tok], pass_sem.at[0], recv_sem.at[head, tok], partner
+            )
+        )
+        sends[-1].start()
+        for i, there in enumerate(others):
+            sends.append(
+                remote(
+                    src_notes.at[there],
+                    out_notes.at[tok],
+                    send_sem.at[peers + i],
+                    note_sem.at[tok],
+                    (there, head),
+                )
+            )
+            sends[-1].start()
+        own = [
+            pltpu.make_async_copy(src.at[tok], out.at[head, tok], own_sem.at[0]),
+            pltpu.make_async_copy(src_notes.at[tok], out_notes.at[tok], own_sem.at[1]),
         ]
-        meet(others)
-        own = pltpu.make_async_copy(src.at[tok], out.at[head, tok], own_sem)
-        own.start()
-        sends = []
-        for i, (there, side) in enumerate(others):
-            copy = pltpu.make_async_remote_copy(
-                src_ref=src.at[there],
-                dst_ref=out.at[head, tok],
-                send_sem=send_sem.at[i],
-                recv_sem=recv_sem.at[head, tok],
-                device_id=(there, side),
-                device_id_type=MESH_ID,
-            )
+        for copy in own:
             copy.start()
-            sends.append(copy)
-        for there, side in others:
-            pltpu.make_async_remote_copy(
-                src_ref=src.at[there],
-                dst_ref=out.at[side, there],
-                send_sem=send_sem.at[0],
-                recv_sem=recv_sem.at[side, there],
-                device_id=(there, side),
-                device_id_type=MESH_ID,
-            ).wait_recv()
+        for i, there in enumerate(others):
+            spot = out.at[head, there]
+            remote(spot, spot, send_sem.at[0], recv_sem.at[head, there], partner).wait_recv()
+            sends.append(
+                remote(spot, spot, pass_sem.at[1 + i], recv_sem.at[head, there], partner)
+            )
+            sends[-1].start()
+        for there in [tok] + others:
+            spot = out.at[1 - head, there]
+            remote(spot, spot, send_sem.at[0], recv_sem.at[1 - head, there], partner).wait_recv()
+        for there in others:
+            spot = out_notes.at[there]
+            remote(spot, spot, send_sem.at[0], note_sem.at[there], partner).wait_recv()
         for copy in sends:
             copy.wait_send()
-        own.wait()
+        for copy in own:
+            copy.wait()
 
     return pl.pallas_call(
         kernel,
-        out_shape=jax.ShapeDtypeStruct((2,) + blocks.shape, blocks.dtype),
-        in_specs=in_vmem(1),
-        out_specs=in_vmem(1)[0],
+        out_shape=[
+            jax.ShapeDtypeStruct((2,) + blocks.shape, blocks.dtype),
+            jax.ShapeDtypeStruct(notes.shape, notes.dtype),
+        ],
+        in_specs=in_vmem(2),
+        out_specs=in_vmem(2),
         scratch_shapes=[
             pltpu.SemaphoreType.DMA((2 * peers,)),
             pltpu.SemaphoreType.DMA((2, peers)),
-            pltpu.SemaphoreType.DMA,
+            pltpu.SemaphoreType.DMA((peers,)),
+            pltpu.SemaphoreType.DMA((peers,)),
+            pltpu.SemaphoreType.DMA((2,)),
         ],
         compiler_params=pltpu.CompilerParams(
             collective_id=number, has_side_effects=True, vmem_limit_bytes=VMEM_LIMIT
         ),
         name="to_owners",
-    )(blocks)
+    )(blocks, notes)
 
 
 def gather_rows(block, peers, number):
@@ -376,18 +415,22 @@
         meet([across_x, across_y, sibling] + along_z)
 
         def spot(z_, y_, core_, x_, h):
-            start = pl.multiple_of(place(z_, y_, core_) * rows + h * half, half)
-            return out.at[pl.ds(start, half), pl.ds(pl.multiple_of(x_ * width, 128), width)]
+            start = place(z_, y_, core_) * rows + (h or 0) * half
+            size = rows if h is None else half
+            return out.at[
+                pl.ds(pl.multiple_of(start, half), size),
+                pl.ds(pl.multiple_of(x_ * width, 128), width),
+            ]
 
         def slot(z_, y_, core_, x_, h):
-            return ((place(z_, y_, core_) * 2) + x_) * 2 + h
+            return (place(z_, y_, core_) * 2 + x_) * 2 + (h or 0)
 
         sends = []
 
         def push(target, z_, y_, core_, x_, h, fresh=False):
             dst = spot(z_, y_, core_, x_, h)
             copy = pltpu.make_async_remote_copy(
-                src_ref=src.at[pl.ds(h * half, half)] if fresh else dst,
+                src_ref=src if fresh else dst,
                 dst_ref=dst,
                 send_sem=send_sem.at[len(sends)],
                 recv_sem=recv_sem.at[slot(z_, y_, core_, x_, h)],
@@ -408,55 +451,46 @@
                 device_id_type=MESH_ID,
             ).wait_recv()
 
-        for target in along_z[:1] + along_z[2:] + along_z[1:2]:
-            for h in range(2):
-                push(target, z, y, core, x, h, True)
-        for h in range(2):
-            push(across_x, z, y, core, x, h, True)
-            push(across_y, z, y, core, x, h, True)
-            push(sibling, z, y, core, x, h, True)
-        own = [
-            pltpu.make_async_copy(
-                src.at[pl.ds(h * half, half)], spot(z, y, core, x, h), own_sem.at[h]
-            )
-            for h in range(2)
-        ]
-        for copy in own:
-            copy.start()
-        turns = [0, 1, 3, 2][:layers]
+        turns = [1, 3, 2][: layers - 1]
+        for d in turns:
+            push(along_z[d - 1], z, y, core, x, None, True)
+        for target in (across_x, across_y, sibling):
+            push(target, z, y, core, x, None, True)
+        own = pltpu.make_async_copy(src, spot(z, y, core, x, None), own_sem)
+        own.start()
+
+        def second(z_):
+            land(z_, 1 - y, core, x, None)
+            push(across_x, z_, 1 - y, core, x, 0)
+            land(z_, y, core, 1 - x, None)
+            push(across_y, z_, y, core, 1 - x, 1)
+            push(sibling, z_, 1 - y, core, x, None)
+            push(sibling, z_, y, core, 1 - x, None)
+
+        def third(z_):
+            land(z_, 1 - y, core, 1 - x, 0)
+            land(z_, 1 - y, core, 1 - x, 1)
+            push(sibling, z_, 1 - y, core, 1 - x, None)
+
         for d in turns:
             z_ = lax.rem(z + d, layers)
-            if d > 0:
-                for h in range(2):
-                    land(z_, y, core, x, h)
-                    push(across_x, z_, y, core, x, h)
-                    push(across_y, z_, y, core, x, h)
-                    push(sibling, z_, y, core, x, h)
-            land(z_, 1 - y, core, x, 0)
-            push(across_x, z_, 1 - y, core, x, 0)
-            push(sibling, z_, 1 - y, core, x, 0)
-            land(z_, y, core, 1 - x, 1)
-            push(across_y, z_, y, core, 1 - x, 1)
-            push(sibling, z_, y, core, 1 - x, 1)
-            land(z_, 1 - y, core, x, 1)
-            push(sibling, z_, 1 - y, core, x, 1)
-            land(z_, y, core, 1 - x, 0)
-            push(sibling, z_, y, core, 1 - x, 0)
+            land(z_, y, core, x, None)
+            for target in (across_x, across_y, sibling):
+                push(target, z_, y, core, x, None)
+            if d == turns[0]:
+                second(z)
         for d in turns:
-            z_ = lax.rem(z + d, layers)
-            for h in range(2):
-                land(z_, 1 - y, core, 1 - x, h)
-                push(sibling, z_, 1 - y, core, 1 - x, h)
-        for d in turns:
+            second(lax.rem(z + d, layers))
+        for d in [0] + turns:
+            third(lax.rem(z + d, layers))
+        for d in [0] + turns:
             z_ = lax.rem(z + d, layers)
             for y_ in (y, 1 - y):
                 for x_ in (x, 1 - x):
-                    for h in range(2):
-                        land(z_, y_, 1 - core, x_, h)
+                    land(z_, y_, 1 - core, x_, None)
         for copy in sends:
             copy.wait_send()
-        for copy in own:
-            copy.wait()
+        own.wait()
 
     return pl.pallas_call(
         kernel,
@@ -464,9 +498,9 @@
         in_specs=in_vmem(1),
         out_specs=in_vmem(1)[0],
         scratch_shapes=[
-            pltpu.SemaphoreType.DMA((128,)),
+            pltpu.SemaphoreType.DMA((64,)),
             pltpu.SemaphoreType.DMA((4 * peers,)),
-            pltpu.SemaphoreType.DMA((2,)),
+            pltpu.SemaphoreType.DMA,
         ],
         compiler_params=pltpu.CompilerParams(
             collective_id=number, has_side_effects=True, vmem_limit_bytes=VMEM_LIMIT
@@ -475,12 +509,15 @@
     )(block)
 
 
-def scatter_sums(parts, peers, number):
+def scatter_sums(parts, back, peers, number):
     layers = parts.shape[3]
     half, full = parts.shape[4:]
     width = full // 2
 
-    def kernel(src, out, got_core, kept, got_first, mid, got_second, last, got_z, sends, recvs):
+    def kernel(
+        src, back_src, out, back_out, got_core, kept, got_first, mid, got_second, last, got_z,
+        sends, recvs, back_sends, back_recvs, own_sem,
+    ):
         tok, x = lax.axis_index("tok"), lax.axis_index("head")
         z, y, core = tok // 4, (tok // 2) % 2, tok % 2
 
@@ -491,7 +528,8 @@
         across_y = (place(z, 1 - y, core), x)
         sibling = (place(z, y, 1 - core), x)
         along_z = [(place(lax.rem(z + d, layers), y, core), x) for d in range(1, layers)]
-        meet([across_x, across_y, sibling] + along_z)
+        others = [lax.rem(tok + d, peers) for d in range(1, peers)]
+        meet([across_x] + [(there, x) for there in others])
 
         def copy_to(target, source, dest, index):
             copy = pltpu.make_async_remote_copy(
@@ -518,6 +556,21 @@
                 cores[h][g] = copy_to(
                     sibling, src.at[h, 1 - core, y_], got_core.at[h, y_], 2 * h + g
                 )
+
+        backs = []
+        for i, there in enumerate(others):
+            copy = pltpu.make_async_remote_copy(
+                src_ref=back_src.at[there],
+                dst_ref=back_out.at[tok],
+                send_sem=back_sends.at[i],
+                recv_sem=back_recvs.at[tok],
+                device_id=(there, x),
+                device_id_type=MESH_ID,
+            )
+            copy.start()
+            backs.append(copy)
+        own = pltpu.make_async_copy(back_src.at[tok], back_out.at[tok], own_sem)
+        own.start()
 
         def fold_core(h, y_):
             @pl.loop(0, layers)
@@ -611,15 +664,31 @@
             for d in range(1, layers):
                 acc = acc + got_z[h, d - 1].astype(jnp.float32)
             out[h] = acc.astype(out.dtype)
+        for there in others:
+            spot = back_out.at[there]
+            pltpu.make_async_remote_copy(
+                src_ref=spot,
+                dst_ref=spot,
+                send_sem=back_sends.at[0],
+                recv_sem=back_recvs.at[there],
+                device_id=sibling,
+                device_id_type=MESH_ID,
+            ).wait_recv()
+        for copy in backs:
+            copy.wait_send()
+        own.wait()
         for copy in cores[0] + cores[1] + first_x + [first_y, second_y, second_x] + zs:
             copy.wait_send()
 
     kind = parts.dtype
     return pl.pallas_call(
         kernel,
-        out_shape=jax.ShapeDtypeStruct((2, half, width), kind),
-        in_specs=in_vmem(1),
-        out_specs=in_vmem(1)[0],
+        out_shape=[
+            jax.ShapeDtypeStruct((2, half, width), kind),
+            jax.ShapeDtypeStruct(back.shape, back.dtype),
+        ],
+        in_specs=in_vmem(2),
+        out_specs=in_vmem(2),
         scratch_shapes=[
             pltpu.VMEM((2, 2, layers, half, full), kind),
             pltpu.VMEM((2, 2, layers, half, full), kind),
@@ -630,17 +699,21 @@
             pltpu.VMEM((2, layers - 1, half, width), kind),
             pltpu.SemaphoreType.DMA((9 + 2 * layers,)),
             pltpu.SemaphoreType.DMA((9 + 2 * layers,)),
+            pltpu.SemaphoreType.DMA((peers,)),
+            pltpu.SemaphoreType.DMA((peers,)),
+            pltpu.SemaphoreType.DMA,
         ],
         compiler_params=pltpu.CompilerParams(
             collective_id=number, has_side_effects=True, vmem_limit_bytes=VMEM_LIMIT
         ),
         name="scatter_sums",
-    )(parts)
+    )(parts, back)
 
 
 def ragged_attend(queries, cache, ids, bounds, base, factor):
     slots, heads, width = queries.shape
-    blocks = cache.shape[0] // KEY_BLOCK
+    blocks = cache.shape[1] // KEY_BLOCK
+    cuts = list(zip(KEY_CUTS[:-1], KEY_CUTS[1:]))
 
     def kernel(ids_ref, bounds_ref, base_ref, q_ref, kv_ref, num_ref, den_ref):
         j = pl.program_id(0)
@@ -650,31 +723,45 @@
             num_ref[...] = jnp.zeros_like(num_ref)
             den_ref[...] = jnp.zeros_like(den_ref)
 
-        kv = kv_ref[...]
-        who = [ids_ref[j * WINDOW + w] for w in range(WINDOW)]
-        some = jnp.concatenate([q_ref[r] for r in who], axis=0)
-        scores = factor * lax.dot_general(
-            some, kv, (((1,), (1,)), ((), ())), preferred_element_type=jnp.float32
-        )
-        places = (
-            base_ref[0]
-            + j * KEY_BLOCK
-            + lax.broadcasted_iota(jnp.int32, (heads, KEY_BLOCK), 1)
-        )
-        inside = jnp.concatenate(
-            [
-                ((places >= bounds_ref[r]) & (places < bounds_ref[slots + r])).astype(jnp.int32)
-                for r in who
-            ],
-            axis=0,
-        )
-        weights = jnp.where(inside > 0, jnp.exp(scores), 0.0).astype(jnp.bfloat16)
-        num = jnp.dot(weights, kv[:, :LATENT], preferred_element_type=jnp.float32)
-        den = jnp.sum(weights.astype(jnp.float32), axis=1, keepdims=True)
-        for w, r in enumerate(who):
-            rows = slice(w * heads, (w + 1) * heads)
-            num_ref[r] += num[rows]
-            den_ref[r] += jnp.broadcast_to(den[rows], (heads, 128))
+        found = []
+        for i, (low, high) in enumerate(cuts):
+            size = high - low
+            kv = kv_ref[:, low:high]
+            who = [ids_ref[(j * len(cuts) + i) * WINDOW + w] for w in range(WINDOW)]
+            some = jnp.concatenate([q_ref[r] for r in who], axis=0)
+            scores = factor * jnp.dot(some, kv, preferred_element_type=jnp.float32)
+            places = (
+                base_ref[0]
+                + j * KEY_BLOCK
+                + low
+                + lax.broadcasted_iota(jnp.int32, (heads, size), 1)
+            )
+            lifted = jnp.exp(scores)
+            weights = jnp.concatenate(
+                [
+                    jnp.where(
+                        (places >= bounds_ref[r]) & (places < bounds_ref[slots + r]),
+                        lifted[w * heads : (w + 1) * heads],
+                        0.0,
+                    )
+                    for w, r in enumerate(who)
+                ],
+                axis=0,
+            ).astype(jnp.bfloat16)
+            num = lax.dot_general(
+                weights,
+                kv[:LATENT],
+                (((1,), (1,)), ((), ())),
+                preferred_element_type=jnp.float32,
+            )
+            wide = weights.astype(jnp.float32)
+            den = sum(wide[:, k : k + 128] for k in range(0, size, 128))
+            found.append((who, num, den))
+        for who, num, den in found:
+            for w, r in enumerate(who):
+                rows = slice(w * heads, (w + 1) * heads)
+                num_ref[r] += num[rows]
+                den_ref[r] += den[rows]
 
     return pl.pallas_call(
         kernel,
@@ -687,7 +774,7 @@
             grid=(blocks,),
             in_specs=[
                 pl.BlockSpec((slots, heads, width), lambda j, *_: (0, 0, 0)),
-                pl.BlockSpec((KEY_BLOCK, width), lambda j, *_: (j, 0)),
+                pl.BlockSpec((width, KEY_BLOCK), lambda j, *_: (0, j)),
             ],
             out_specs=[
                 pl.BlockSpec((slots, heads, LATENT), lambda j, *_: (0, 0, 0)),
@@ -749,13 +836,14 @@
         ],
         axis=1,
     ).astype(bf16)
-    meta = jnp.pad(meta, ((0, 0), (0, part - meta.shape[1])))
-    sent = pick_rows(placed, jnp.concatenate([hidden, meta], axis=1))
-    blocks = sent.reshape(peers, each, 2, part).transpose(0, 2, 1, 3)
-    blocks = blocks.reshape(peers, 2 * each * part // 128, 128)
-    arrived = to_owners(blocks, 0).reshape(2, peers, 2, each, part)
-    wide = arrived[:, :, 0].reshape(2, rows, part)
-    meta = arrived[0, :, 1].reshape(rows, part)[:, : 3 + expert_count].astype(jnp.int32)
+    meta = jnp.pad(meta, ((0, 0), (0, 128 // each - meta.shape[1])))
+    sent_meta = jnp.dot(placed.astype(bf16), meta, preferred_element_type=f32)
+    blocks = pick_rows(placed, hidden).reshape(peers, each * part // 128, 128)
+    wide, meta = to_owners(
+        blocks, sent_meta.astype(jnp.int32).reshape(peers, 1, 128), 0
+    )
+    wide = wide.reshape(2, rows, part)
+    meta = meta.reshape(rows, 128 // each)[:, : 3 + expert_count]
     slot, lengths = meta[:, 0], meta[:, 1] * 64 + meta[:, 2]
     mask = meta[:, 3:]
     starts = jnp.sum(jnp.where(slot[None, :] < slot[:, None], lengths[None, :], 0), axis=1)
@@ -789,7 +877,11 @@
     self_weight = jnp.exp(self_score).astype(bf16).astype(f32)
 
     key_rows = latent_cache.shape[0]
-    block_starts = head * key_rows + jnp.arange(0, key_rows, KEY_BLOCK, dtype=jnp.int32)
+    block_starts = (
+        head * key_rows
+        + jnp.arange(0, key_rows, KEY_BLOCK, dtype=jnp.int32)[:, None]
+        + jnp.array(KEY_CUTS[:-1], jnp.int32)
+    ).reshape(-1)
     ends = starts + lengths
     first = jnp.sum((ends[None, :] <= block_starts[:, None]).astype(jnp.int32), axis=1)
     first = jnp.minimum(first, rows - WINDOW)
@@ -799,13 +891,13 @@
     )
     numerator, denominator = ragged_attend(
         jnp.concatenate([probes, far_probes], axis=1),
-        latent_cache,
+        latent_cache.T,
         window_ids.reshape(-1).astype(jnp.int32),
         jnp.concatenate([starts, ends]).astype(jnp.int32),
         (head * key_rows).reshape(1).astype(jnp.int32),
         factor,
     )
-    denominator = denominator[:, :, 0]
+    denominator = jnp.sum(denominator, axis=2)
     far_num, far_den = swap_pair(
         [
             numerator[:, local_heads:].astype(bf16).reshape(rows * local_heads, LATENT),
@@ -838,10 +930,6 @@
     notes = jnp.concatenate([high, low, mask.astype(bf16)], axis=1)
     notes = jnp.pad(notes, ((0, 0), (0, 128 - notes.shape[1])))
     gathered = gather_rows(jnp.concatenate([gained, notes], axis=1), peers, 4)
-
-    back = jnp.concatenate([attended, new_entry], axis=1).reshape(peers, each, -1)
-    back = lax.all_to_all(back, "tok", split_axis=0, concat_axis=0, tiled=True)
-    back = pick_rows(placed.T, back.reshape(rows, -1))
 
     span = part + 128
     tokens = jnp.concatenate([gathered[:, :part], gathered[:, span : span + part]], axis=1)
@@ -872,9 +960,16 @@
     weight = jnp.sum(jnp.where(moved, weight[None, :], 0.0), axis=1)
     terms = jnp.dot(activity, expert_down[0], preferred_element_type=f32) * weight[:, None]
     terms = terms.astype(bf16).reshape(2, 2, 2, layers, half, 2 * part)
-    summed = scatter_sums(terms, peers, 5).reshape(rows, part)
-    expert_mix = pick_rows(placed.T, summed)
-    return (back[:, part:], back[:, :part], expert_mix)
+    back = jnp.concatenate([attended, new_entry], axis=1)
+    back = jnp.pad(back, ((0, 0), (0, 2 * part - back.shape[1])))
+    summed, back = scatter_sums(terms, back.reshape(peers, each * 2 * part // 128, 128), peers, 5)
+    mixed_back = jnp.concatenate([back.reshape(rows, 2 * part), summed.reshape(rows, part)], axis=1)
+    final = pick_rows(placed.T, mixed_back)
+    return (
+        final[:, part : part + LATENT + ROPE],
+        final[:, :part],
+        final[:, 2 * part :],
+    )
 
 
 def solution(mesh):

time: 167 us -> 142 us (0.85)
  Pallas kernels: 97.3 us -> 85.4 us
  local copies, waits for them, and re-layouts: 21.2 us -> 12.8 us
  starting transfers between devices: 6.45 us -> 0 us
  other arithmetic: 10.5 us -> 14.8 us
  matrix products: 29.1 us -> 26.6 us
    pallas_call x1, Pallas kernels: 25.9 us -> 17.6 us  [gather_rows(): pl.pallas_call(kernel, out_shape=jax.ShapeDtypeStruct((rows * peers, 2 *...]
    all_to_all x1 -> x0, starting transfers between devices: 6.45 us -> none  [direct_body(): back = lax.all_to_all(back, 'tok', split_axis=0, concat_axis=0, tiled=True)]
    unnamed x43 -> x54, local copies, waits for them, and re-layouts: 11.6 us -> 5.13 us
    pallas_call x1, Pallas kernels: 11.5 us -> 6.48 us  [ragged_attend(): pl.pallas_call(kernel, out_shape=[jax.ShapeDtypeStruct((slots, heads, LAT...]
    pallas_call x2, Pallas kernels: 35.4 us -> 37.8 us  [the longest x1 24.5 us: scatter_sums(): pl.pallas_call(kernel, out_shape=[jax.ShapeDtypeStruct((2, half, width),...]
    dot_general x1, matrix products: 4.63 us -> 2.8 us  [direct_body(): jnp.dot(tokens, expert_gate[0], preferred_element_type=f32) * inv_ffn]
    dot_general x4 -> x3, matrix products: 7.99 us -> 7.16 us  [pick_rows(): jnp.dot(chosen.astype(jnp.bfloat16), values, preferred_element_type=jnp.f...]
  transfers between devices with their start and end apart: 1 -> 0, of which waited for: 0 -> 0; matrix products, arithmetic and copies ran while one was open for 11% -> 0% of each run, Pallas kernels for 29% -> 0%
where the time goes in v2:
time: 142 us; the launch traced here: 141 us
  Pallas kernels  85.4 us (60%)
  matrix products  26.6 us (19%)
  other arithmetic  14.8 us (10%)
  local copies, waits for them, and re-layouts  12.8 us (9%)
    pallas_call x1, Pallas kernels, scatter_sums(): pl.pallas_call(kernel, out_shape=[jax.ShapeDtypeStruct((2, half, width),...  24.5 us
    pallas_call x3, Pallas kernels, swap_pair(): pl.pallas_call(kernel, out_shape=[jax.ShapeDtypeStruct(a.shape, a.dtype)...  23.6 us
    pallas_call x1, Pallas kernels, gather_rows(): pl.pallas_call(kernel, out_shape=jax.ShapeDtypeStruct((rows * peers, 2 *...  17.6 us
    pallas_call x1, Pallas kernels, to_owners(): pl.pallas_call(kernel, out_shape=[jax.ShapeDtypeStruct((2,) + blocks.shap...  13.3 us
    dot_general x3, matrix products, pick_rows(): jnp.dot(chosen.astype(jnp.bfloat16), values, preferred_element_type=jnp.f...  7.16 us
    pallas_call x1, Pallas kernels, ragged_attend(): pl.pallas_call(kernel, out_shape=[jax.ShapeDtypeStruct((slots, heads, LAT...  6.48 us
    unnamed x54, local copies, waits for them, and re-layouts  5.13 us
    dot_general x1, matrix products, direct_body(): queries = jnp.dot(normed, w_query, preferred_element_type=f32).astype(bf16)  3.92 us

profile of v2, /device:TPU:0, one launch (start us, length us, event | category | flops | bytes accessed | tf_op | source)
XLA Modules:
  0.0 141.0 jit_solution(1434383814119030156)
XLA Ops:
  0.6 0.8 fusion.119
  1.7 0.7 convert_bitcast_fusion
  2.3 0.7 convert_reduce_fusion
  3.3 1.0 convolution_convert_fusion.4
  4.3 13.3 %to_owners.1 = (bf16[2,16,16,128]{3,2,1,0:T(8,128)(2,1)S(1)}, s32[16,1,128]{2,1,0:T(1,128)S(1)}) custom-call(bf16[16,16,128]{2,1,0:T(8,128)(2,1)S(1)} %reshape.361.src, s32[16,1,128]{2,1,0:T(1,128)S(1)} %reshape.362.src_notes), custom_call_target="tpu_custom_call" | custom-call | tf_op jit(solution)/shard_map/to_owners/pallas_call | solution.py:377
  17.6 0.6 copy-done.3
  18.4 0.8 fusion.28
  19.2 3.9 %convolution_convert_fusion.1 = bf16[32,1536]{1,0:T(8,128)(2,1)S(1)} fusion(bf16[32,2048]{1,0:T(8,128)(2,1)S(1)} %fusion.28, bf16[2048,1536]{1,0:T(8,128)(2,1)} %param.19), kind=kOutput, calls=%fused_computation.7 | convolution fusion | flops 201375744 | bytes 6520832 | tf_op jit(solution)/shard_map/dot_general | solution.py:857
  23.4 0.5 broadcast.516
  23.9 0.7 reduce.11
  25.0 0.6 fusion.136
  25.9 1.5 %fusion.48 = bf16[8,32,512]{2,1,0:T(8,128)(2,1)S(1)} fusion(bf16[8,128,512]{2,1,0:T(8,128)(2,1)} %param.21, bf16[32,8,128]{2,1,0:T(8,128)(2,1)S(1)} %slice.143), kind=kOutput, calls=%fused_computation.71 | convolution fusion | flops 33554432 | bytes 1376256 | tf_op jit(solution)/shard_map/bhn,hnl->bhl/dot_general | solution.py:859
  27.6 0.7 copy-done.6
  28.5 1.8 %fusion.50.refs_1_ = f32[32,576]{1,0:T(8,128)S(1)} fusion(bf16[1024,576]{0,1:T(8,128)(2,1)} %param.20, bf16[32,2048]{1,0:T(8,128)(2,1)S(1)} %fusion.28, s32[]{:T(128)S(6)} %select_n.158), kind=kOutput, calls=%fused_computation.75 | convolution fusion | flops 37748736 | bytes 1318916 | tf_op jit(solution)/shard_map/dot_general | solution.py:856
  30.2 11.3 %swap_pair_1.1 = (bf16[32,8,576]{2,1,0:T(8,128)(2,1)S(1)}, f32[32,576]{1,0:T(8,128)S(1)}) custom-call(bf16[32,8,576]{2,1,0:T(8,128)(2,1)S(1)} %pad_maximum_fusion.6.refs_0_, f32[32,576]{1,0:T(8,128)S(1)} %fusion.50.refs_1_), custom_call_target="tpu_custom_call" | custom-call | tf_op jit(solution)/shard_map/swap_pair_1/pallas_call | solution.py:292
  41.6 0.7 fusion.132
  42.8 0.9 fusion.43
  43.9 0.7 broadcast_add_fusion
  44.6 1.4 add.311
  45.9 0.9 convert_reduce_fusion.3
  46.9 1.0 select_reduce_fusion.1
  47.9 0.8 reshape.365.ids_ref
  48.7 6.5 %ragged_attend.1 = (f32[32,16,512]{2,1,0:T(8,128)S(1)}, f32[32,16,128]{2,1,0:T(8,128)S(1)}) custom-call(s32[60]{0:T(128)S(1)} %reshape.365.ids_ref, s32[64]{0:T(128)S(1)} %pad_add_fusion.bounds_ref, s32[1]{0:T(128)} %bitcast.4.base_ref, bf16[32,16,576]{2,1,0:T(8,128)(2,1)S(1)} %pad_maximum_fusion.5.q_ref, bf16[576,4992]{1,0:T(8,128)(2,1)} %bitcast.71), custom_call_target="tpu_custom_call" | custom-call | tf_op jit(solution)/shard_map/ragged_attend/pallas_call | solution.py:766
  55.2 1.0 copy-done.2
  56.2 1.1 reduce_sum.104
  57.5 7.3 %swap_pair_2.1 = (bf16[256,512]{1,0:T(8,128)(2,1)S(1)}, f32[2,128]{1,0:T(2,128)S(1)}) custom-call(bf16[256,512]{1,0:T(8,128)(2,1)S(1)} %fusion.30.refs_0_, f32[2,128]{1,0:T(2,128)S(1)} %reshape.369.refs_1_), custom_call_target="tpu_custom_call" | custom-call | tf_op jit(solution)/shard_map/swap_pair_2/pallas_call | solution.py:292
  64.8 0.7 fusion.81
  65.6 1.2 fusion.24
  66.8 1.5 %fusion.19 = bf16[8,4,8,128]{3,2,1,0:T(8,128)(2,1)S(1)} fusion(bf16[8,512,128]{2,1,0:T(8,128)(2,1)} %param.22, bf16[32,8,512]{2,1,0:T(8,128)(2,1)S(1)} %fusion.24), kind=kOutput, calls=%fused_computation.16 | convolution fusion | flops 33587200 | bytes 1376256 | tf_op jit(solution)/shard_map/bhl,hld->bhd/dot_general | solution.py:915
  68.4 3.1 %fusion.45 = f32[32,2048]{1,0:T(8,128)S(1)} fusion(bf16[1024,2048]{1,0:T(8,128)(2,1)} %param.23, bf16[8,4,8,128]{3,2,1,0:T(8,128)(2,1)S(1)} %fusion.19), kind=kOutput, calls=%fused_computation.67 | convolution fusion | flops 134217728 | bytes 4521984 | tf_op jit(solution)/shard_map/dot_general | solution.py:917
  71.5 5.0 %swap_pair_3.1 = f32[32,1024]{1,0:T(8,128)S(1)} custom-call(f32[32,1024]{1,0:T(8,128)S(1)} %constant_dynamic-slice_fusion.refs_0_), custom_call_target="tpu_custom_call" | custom-call | tf_op jit(solution)/shard_map/swap_pair_3/pallas_call | solution.py:292
  76.5 0.7 reshape.363
  77.2 1.0 fusion.41
  78.4 0.9 fusion.137
  79.7 17.6 %gather_rows.1 = bf16[512,2304]{1,0:T(8,128)(2,1)S(1)} custom-call(bf16[32,1152]{1,0:T(8,128)(2,1)S(1)} %pad_maximum_fusion.8.src), custom_call_target="tpu_custom_call" | custom-call | tf_op jit(solution)/shard_map/gather_rows/pallas_call | solution.py:495
  97.4 1.4 copy-done.1
  99.2 0.4 fusion.130
  99.7 0.3 select_reduce_fusion
  99.9 1.9 %fusion.133 = (bf16[512,1024]{1,0:T(8,128)(2,1)S(1)}, bf16[512,1024]{1,0:T(8,128)(2,1)S(1)}) fusion(bf16[512,2304]{1,0:T(8,128)(2,1)} %copy-done.1), kind=kLoop, calls=%fused_computation.227 | loop fusion | bytes 4194304 | tf_op jit(solution)/shard_map/slice | solution.py:935
  101.8 1.0 copy-done.8
  102.8 0.3 copy-done.9
  103.1 2.8 %fusion.5 = f32[512,704]{0,1:T(8,128)} fusion(bf16[1,2048,704]{1,2,0:T(8,128)(2,1)S(1)} %copy-done.26, bf16[512,1024]{1,0:T(8,128)(2,1)S(1)} %get-tuple-element.34, bf16[512,1024]{1,0:T(8,128)(2,1)S(1)} %get-tuple-element.33, f32[512]{0:T(512)S(1)} %fusion.34), kind=kOutput, calls=%fused_computation.9 | convolution fusion | flops 1480949760 | bytes 6424576 | tf_op jit(solution)/shard_map/dot_general | solution.py:943
  105.9 5.9 %convolution_convert_fusion.2 = bf16[512,704]{0,1:T(8,128)(2,1)} fusion(bf16[1,2048,704]{1,2,0:T(8,128)(2,1)} %param.31, f32[512,704]{0,1:T(8,128)} %fusion.5, bf16[512,1024]{1,0:T(8,128)(2,1)} %copy-done.9, bf16[512,1024]{1,0:T(8,128)(2,1)} %copy-done.8, f32[512]{0:T(512)S(1)} %fusion.34, s32[512]{0:T(512)S(1)} %fusion.98), kind=kOutput, calls=%fused_computation.13 | convolution fusion | flops 1852833792 | bytes 7147520 | tf_op jit(solution)/shard_map/dot_general | solution.py:790
  111.9 2.9 %multiply_convert_fusion = bf16[512,2048]{1,0:T(8,128)(2,1)S(1)} fusion(bf16[512,704]{0,1:T(8,128)(2,1)} %convolution_convert_fusion.2, bf16[1,704,2048]{2,1,0:T(8,128)(2,1)S(1)} %copy-done, f32[512]{0:T(512)S(1)} %select_reduce_fusion), kind=kOutput, calls=%fused_computation | convolution fusion | flops 1478492160 | bytes 5703680 | tf_op jit(solution)/shard_map/dot_general | solution.py:961
  114.8 24.5 %scatter_sums.1 = (bf16[2,16,1024]{2,1,0:T(8,128)(2,1)S(1)}, bf16[16,32,128]{2,1,0:T(8,128)(2,1)S(1)}) custom-call(bf16[2,2,2,4,16,2048]{5,4,3,2,1,0:T(8,128)(2,1)S(1)} %bitcast.69, bf16[16,32,128]{2,1,0:T(8,128)(2,1)S(1)} %reshape.373.back_src), custom_call_target="tpu_custom_call" | custom-call | tf_op jit(solution)/shard_map/scatter_sums/pallas_call | solution.py:684
  139.4 0.2 convolution_convert_fusion
  139.7 0.7 fusion.134
  140.3 0.6 slice.161
  (104 shorter events, 4.1 us)
Async XLA Ops:
  0.6 111.2 %copy-start = (bf16[1,704,2048]{2,1,0:T(8,128)(2,1)S(1)}, bf16[1,704,2048]{2,1,0:T(8,128)(2,1)}, u32[]{:S(2)}) copy-start(bf16[1,704,2048]{2,1,0:T(8,128)(2,1)} %param.32) | copy-start | bytes 8650756
  1.6 2.6 %copy-start.21 = (s32[32]{0:T(128)}, s32[32]{0:T(128)S(1)}, u32[]{:S(2)}) copy-start(s32[32]{0:T(128)S(1)} %multiply_add_fusion.1) | copy-start | bytes 388
  17.6 0.6 copy-start.3
  24.6 17.7 %copy-start.10 = (s32[32,64]{1,0:T(8,128)}, s32[32,64]{1,0:T(8,128)S(1)}, u32[]{:S(2)}) copy-start(s32[32,64]{1,0:T(8,128)S(1)} %reshape.364) | copy-start | bytes 24580
  25.0 2.6 %copy-start.23 = (s32[32]{0:T(128)}, s32[32]{0:T(128)S(1)}, u32[]{:S(2)}) copy-start(s32[32]{0:T(128)S(1)} %select_reduce_fusion.2) | copy-start | bytes 388
  25.9 2.5 %copy-start.12 = (bf16[32,8,32]{2,1,0:T(8,128)(2,1)}, bf16[32,8,32]{2,1,0:T(8,128)(2,1)S(1)}, u32[]{:S(2)}) copy-start(bf16[32,8,32]{2,1,0:T(8,128)(2,1)S(1)} %get-tuple-element.37) | copy-start | bytes 49156
  25.9 2.5 %copy-start.14 = (bf16[32,8,32]{2,1,0:T(8,128)(2,1)}, bf16[32,8,32]{2,1,0:T(8,128)(2,1)S(1)}, u32[]{:S(2)}) copy-start(bf16[32,8,32]{2,1,0:T(8,128)(2,1)S(1)} %get-tuple-element.38) | copy-start | bytes 49156
  27.6 0.7 copy-start.6
  28.4 15.3 %copy-start.7 = (bf16[8,32,512]{2,0,1:T(8,128)(2,1)S(1)}, bf16[8,32,512]{2,0,1:T(8,128)(2,1)}, u32[]{:S(2)}) copy-start(bf16[8,32,512]{2,0,1:T(8,128)(2,1)} %copy-done.6) | copy-start | bytes 786436
  28.4 15.3 %copy-start.13 = (bf16[32,8,32]{2,1,0:T(8,128)(2,1)S(1)}, bf16[32,8,32]{2,1,0:T(8,128)(2,1)}, u32[]{:S(2)}) copy-start(bf16[32,8,32]{2,1,0:T(8,128)(2,1)} %copy-done.12) | copy-start | bytes 49156
  28.4 15.3 %copy-start.15 = (bf16[32,8,32]{2,1,0:T(8,128)(2,1)S(1)}, bf16[32,8,32]{2,1,0:T(8,128)(2,1)}, u32[]{:S(2)}) copy-start(bf16[32,8,32]{2,1,0:T(8,128)(2,1)} %copy-done.14) | copy-start | bytes 49156
  28.4 15.4 %copy-start.24 = (s32[32]{0:T(128)S(1)}, s32[32]{0:T(128)}, u32[]{:S(2)}) copy-start(s32[32]{0:T(128)} %copy-done.23) | copy-start | bytes 388
  28.4 15.4 %copy-start.25 = (s32[32]{0:T(128)S(1)}, s32[32]{0:T(128)}, u32[]{:S(2)}) copy-start(s32[32]{0:T(128)} %get-tuple-element.48) | copy-start | bytes 388
  42.3 1.3 copy-start.16
  42.7 1.1 copy-start.18
  55.1 1.0 copy-start.2
  55.2 1.1 copy-start.5
  68.3 8.2 %copy-start.4 = (bf16[2,16,16,128]{3,2,1,0:T(8,128)(2,1)S(1)}, bf16[2,16,16,128]{3,2,1,0:T(8,128)(2,1)}, u32[]{:S(2)}) copy-start(bf16[2,16,16,128]{3,2,1,0:T(8,128)(2,1)} %copy-done.3) | copy-start | bytes 393220
  68.3 9.8 %copy-start.17 = (bf16[32,512]{1,0:T(8,128)(2,1)S(1)}, bf16[32,512]{1,0:T(8,128)(2,1)}, u32[]{:S(2)}) copy-start(bf16[32,512]{1,0:T(8,128)(2,1)} %copy-done.16) | copy-start | bytes 98308
  68.3 9.8 %copy-start.19 = (bf16[32,32]{1,0:T(8,128)(2,1)S(1)}, bf16[32,32]{1,0:T(8,128)(2,1)}, u32[]{:S(2)}) copy-start(bf16[32,32]{1,0:T(8,128)(2,1)} %copy-done.18) | copy-start | bytes 6148
  68.4 10.0 %copy-start.20 = (f32[1024]{0:T(1024)S(1)}, f32[1024]{0:T(1024)}, u32[]{:S(2)}) copy-start(f32[1024]{0:T(1024)} %param.27) | copy-start | bytes 12292
  71.4 8.1 %copy-start.11 = (s32[32,64]{1,0:T(8,128)S(1)}, s32[32,64]{1,0:T(8,128)}, u32[]{:S(2)}) copy-start(s32[32,64]{1,0:T(8,128)} %copy-done.10) | copy-start | bytes 24580
  97.4 1.4 %copy-start.1 = (bf16[512,2304]{1,0:T(8,128)(2,1)}, bf16[512,2304]{1,0:T(8,128)(2,1)S(1)}, u32[]{:S(2)}) copy-start(bf16[512,2304]{1,0:T(8,128)(2,1)S(1)} %gather_rows.1) | copy-start | bytes 7077892
  99.9 3.2 %copy-start.26 = (bf16[1,2048,704]{1,2,0:T(8,128)(2,1)S(1)}, bf16[1,2048,704]{1,2,0:T(8,128)(2,1)}, u32[]{:S(2)}) copy-start(bf16[1,2048,704]{1,2,0:T(8,128)(2,1)} %param.30) | copy-start | bytes 8650756
  101.8 1.0 copy-start.8
  101.8 1.3 copy-start.9
  114.8 24.6 %copy-start.22 = (s32[32]{0:T(128)S(1)}, s32[32]{0:T(128)}, u32[]{:S(2)}) copy-start(s32[32]{0:T(128)} %copy-done.21) | copy-start | bytes 388

commit v3 on v2

--- a/solution.py
+++ b/solution.py
@@ -396,12 +396,18 @@
     )(blocks, notes)
 
 
-def gather_rows(block, peers, number):
+def gather_experts(block, gate, up, down, order, select, peers, number):
     rows, width = block.shape
     half = rows // 2
     layers = peers // 4
-
-    def kernel(src, out, send_sem, recv_sem, own_sem):
+    part = width - 128
+    units, full = gate.shape
+    some = rows * peers // 2
+
+    def kernel(
+        src, gate_any, up_any, down_any, order_ref, select_ref, terms, out,
+        gate_ref, up_ref, down_ref, send_sem, recv_sem, own_sem, weight_sem,
+    ):
         tok, x = lax.axis_index("tok"), lax.axis_index("head")
         z, y, core = tok // 4, (tok // 2) % 2, tok % 2
 
@@ -458,6 +464,14 @@
             push(target, z, y, core, x, None, True)
         own = pltpu.make_async_copy(src, spot(z, y, core, x, None), own_sem)
         own.start()
+        weights = [
+            pltpu.make_async_copy(a, b, weight_sem.at[i])
+            for i, (a, b) in enumerate(
+                [(gate_any, gate_ref), (up_any, up_ref), (down_any, down_ref)]
+            )
+        ]
+        for copy in weights:
+            copy.start()
 
         def second(z_):
             land(z_, 1 - y, core, x, None)
@@ -479,34 +493,78 @@
                 push(target, z_, y, core, x, None)
             if d == turns[0]:
                 second(z)
-        for d in turns:
-            second(lax.rem(z + d, layers))
-        for d in [0] + turns:
-            third(lax.rem(z + d, layers))
-        for d in [0] + turns:
-            z_ = lax.rem(z + d, layers)
-            for y_ in (y, 1 - y):
-                for x_ in (x, 1 - x):
-                    land(z_, y_, 1 - core, x_, None)
+        near = z + 1 - 2 * (z % 2)
+        pairs = [(z, near), (lax.rem(z + 2, layers), lax.rem(near + 2, layers))]
+        second(near)
+        for z_ in pairs[1]:
+            second(z_)
+
+        def across(a, b):
+            return lax.dot_general(
+                a, b, (((1,), (1,)), ((), ())), preferred_element_type=jnp.float32
+            )
+
+        def product(a, b):
+            return jnp.dot(a, b, preferred_element_type=jnp.float32)
+
+        def expert(group):
+            at = pl.ds(pl.multiple_of(group * some, some), some)
+            left, right = out[at, part:width], out[at, width + part :]
+            logits = product(left, select_ref[:, :128]) + product(right, select_ref[:, :128])
+            named = product(left, select_ref[:, 128:256])
+            squares = product(left, select_ref[:, 256:]) + product(right, select_ref[:, 256:])
+            inv_ffn = lax.rsqrt(squares / full + NORM_EPS)
+            lifted = jnp.where(named > 0.5, jnp.exp(logits * inv_ffn), 0.0)
+            lane = lax.broadcasted_iota(jnp.int32, (some, 128), 1)
+            mine = jnp.sum(jnp.where(lane == tok, lifted, 0.0), axis=1, keepdims=True)
+            weight = mine / jnp.sum(lifted, axis=1, keepdims=True)
+            inv_ffn = inv_ffn[:, :1]
+            first, last = out[at, :part], out[at, width : width + part]
+            gate_value = across(first, gate_ref[:, :part]) + across(last, gate_ref[:, part:])
+            gate_value = gate_value * inv_ffn
+            up_value = across(first, up_ref[:, :part]) + across(last, up_ref[:, part:])
+            up_value = up_value * (inv_ffn * weight)
+            activity = gate_value / (1.0 + jnp.exp(-gate_value)) * up_value
+            moved = product(order_ref[...], activity.astype(out.dtype)).astype(out.dtype)
+            for k in range(0, full, 512):
+                piece = product(moved, down_ref[:, k : k + 512]).astype(terms.dtype)
+                terms[group, :, :, k : k + 512] = piece.reshape(peers, half, 512)
+
+        for g, pair in enumerate(pairs):
+            for z_ in pair:
+                third(z_)
+            for z_ in pair:
+                for y_ in (y, 1 - y):
+                    for x_ in (x, 1 - x):
+                        land(z_, y_, 1 - core, x_, None)
+            if g == 0:
+                own.wait()
+                for copy in weights:
+                    copy.wait()
+            expert(pair[0] // 2)
         for copy in sends:
             copy.wait_send()
-        own.wait()
 
     return pl.pallas_call(
         kernel,
-        out_shape=jax.ShapeDtypeStruct((rows * peers, 2 * width), block.dtype),
-        in_specs=in_vmem(1),
+        out_shape=jax.ShapeDtypeStruct((2, peers, half, full), block.dtype),
+        in_specs=in_vmem(1) + [pl.BlockSpec(memory_space=pl.ANY)] * 3 + in_vmem(2),
         out_specs=in_vmem(1)[0],
         scratch_shapes=[
+            pltpu.VMEM((rows * peers, 2 * width), block.dtype),
+            pltpu.VMEM((units, full), block.dtype),
+            pltpu.VMEM((units, full), block.dtype),
+            pltpu.VMEM((units, full), block.dtype),
             pltpu.SemaphoreType.DMA((64,)),
             pltpu.SemaphoreType.DMA((4 * peers,)),
             pltpu.SemaphoreType.DMA,
+            pltpu.SemaphoreType.DMA((3,)),
         ],
         compiler_params=pltpu.CompilerParams(
             collective_id=number, has_side_effects=True, vmem_limit_bytes=VMEM_LIMIT
         ),
-        name="gather_rows",
-    )(block)
+        name="gather_experts",
+    )(block, gate, up, down, order, select)
 
 
 def scatter_sums(parts, back, peers, number):
@@ -929,37 +987,39 @@
     low = (notes - high.astype(f32)).astype(bf16)
     notes = jnp.concatenate([high, low, mask.astype(bf16)], axis=1)
     notes = jnp.pad(notes, ((0, 0), (0, 128 - notes.shape[1])))
-    gathered = gather_rows(jnp.concatenate([gained, notes], axis=1), peers, 4)
-
-    span = part + 128
-    tokens = jnp.concatenate([gathered[:, :part], gathered[:, span : span + part]], axis=1)
-    marks = gathered[:, part:span].astype(f32), gathered[:, span + part :].astype(f32)
-    count = 1 + expert_count
-    sums = sum(m[:, :count] + m[:, count : 2 * count] for m in marks)
-    inv_ffn = lax.rsqrt(sums[:, :1] / (2 * part) + NORM_EPS)
-    lifted = jnp.exp(sums[:, 1:] * inv_ffn) * marks[0][:, 2 * count : 2 * count + expert_count]
-    here = (jnp.arange(expert_count, dtype=jnp.int32) == tok).astype(f32)
-    weight = jnp.sum(lifted * here, axis=1) / jnp.sum(lifted, axis=1)
-    gate_value = jnp.dot(tokens, expert_gate[0], preferred_element_type=f32) * inv_ffn
-    up_value = jnp.dot(tokens, expert_up[0], preferred_element_type=f32) * inv_ffn
-    activity = (jax.nn.silu(gate_value) * up_value).astype(bf16)
-    every = jnp.arange(rows * peers, dtype=jnp.int32)
     half = rows // 2
     layers = peers // 4
-    h_, c_, y_, z_ = (
-        every // (half * peers),
-        every // (half * peers // 2) % 2,
+    every = jnp.arange(half * peers, dtype=jnp.int32)
+    c_, y_, z_ = (
+        every // (half * peers // 2),
         every // (half * layers) % 2,
         every // half % layers,
     )
-    device = z_ * 4 + y_ * 2 + c_
-    inner = h_ * half + every % half
-    source = inner // each * rows + device * each + inner % each
-    moved = source[:, None] == every[None, :]
-    activity = pick_rows(moved, activity)
-    weight = jnp.sum(jnp.where(moved, weight[None, :], 0.0), axis=1)
-    terms = jnp.dot(activity, expert_down[0], preferred_element_type=f32) * weight[:, None]
-    terms = terms.astype(bf16).reshape(2, 2, 2, layers, half, 2 * part)
+    inner = every % half
+    source = inner // each * rows + (z_ * 4 + y_ * 2 + c_) * each + inner % each
+    order = (source[:, None] == every[None, :]).astype(bf16)
+    count = 1 + expert_count
+    line = jnp.arange(128, dtype=jnp.int32)[:, None]
+    lane = jnp.arange(128, dtype=jnp.int32)[None, :]
+    held = lane < expert_count
+    select = jnp.concatenate(
+        [
+            held & ((line == 1 + lane) | (line == count + 1 + lane)),
+            held & (line == 2 * count + lane),
+            ((line == 0) | (line == count)) & (lane >= 0),
+        ],
+        axis=1,
+    ).astype(bf16)
+    terms = gather_experts(
+        jnp.concatenate([gained, notes], axis=1),
+        expert_gate[0].T,
+        expert_up[0].T,
+        expert_down[0],
+        order,
+        select,
+        peers,
+        4,
+    ).reshape(2, 2, 2, layers, half, 2 * part)
     back = jnp.concatenate([attended, new_entry], axis=1)
     back = jnp.pad(back, ((0, 0), (0, 2 * part - back.shape[1])))
     summed, back = scatter_sums(terms, back.reshape(peers, each * 2 * part // 128, 128), peers, 5)

time: 142 us -> 117 us (0.82)
  matrix products: 26.6 us -> 11.1 us
  local copies, waits for them, and re-layouts: 12.8 us -> 5.16 us
  other arithmetic: 14.8 us -> 7.25 us
  Pallas kernels: 85.4 us -> 91.8 us
    dot_general x3 -> x2, matrix products: 7.16 us -> 1.23 us  [pick_rows(): jnp.dot(chosen.astype(jnp.bfloat16), values, preferred_element_type=jnp.f...]
    dot_general x2 -> x0, matrix products: 5.74 us -> none  [the longest x1 2.94 us: direct_body(): jnp.dot(activity, expert_down[0], preferred_element_type=f32)]
    pallas_call x1, Pallas kernels: 17.6 us -> 22.7 us  [gather_experts(): pl.pallas_call(kernel, out_shape=jax.ShapeDtypeStruct((2, peers, half, fu...]
    unnamed x54 -> x10, local copies, waits for them, and re-layouts: 5.13 us -> 1.84 us
    slice x1 -> x0, local copies, waits for them, and re-layouts: 1.87 us -> none  [direct_body(): gathered[:, :part]]
where the time goes in v3:
time: 117 us; the launch traced here: 116 us
  Pallas kernels  91.8 us (78%)
  matrix products  11.1 us (9%)
  other arithmetic  7.25 us (6%)
  local copies, waits for them, and re-layouts  5.16 us (4%)
    pallas_call x1, Pallas kernels, scatter_sums(): pl.pallas_call(kernel, out_shape=[jax.ShapeDtypeStruct((2, half, width),...  25.8 us
    pallas_call x3, Pallas kernels, swap_pair(): pl.pallas_call(kernel, out_shape=[jax.ShapeDtypeStruct(a.shape, a.dtype)...  23.6 us
    pallas_call x1, Pallas kernels, gather_experts(): pl.pallas_call(kernel, out_shape=jax.ShapeDtypeStruct((2, peers, half, fu...  22.7 us
    pallas_call x1, Pallas kernels, to_owners(): pl.pallas_call(kernel, out_shape=[jax.ShapeDtypeStruct((2,) + blocks.shap...  13.3 us
    pallas_call x1, Pallas kernels, ragged_attend(): pl.pallas_call(kernel, out_shape=[jax.ShapeDtypeStruct((slots, heads, LAT...  6.48 us
    dot_general x1, matrix products, direct_body(): queries = jnp.dot(normed, w_query, preferred_element_type=f32).astype(bf16)  4.02 us
    dot_general x1, matrix products, direct_body(): piece = jnp.dot(head_out, w_out, preferred_element_type=f32)  3.02 us

profile of v3, /device:TPU:0, one launch (start us, length us, event | category | flops | bytes accessed | tf_op | source)
XLA Modules:
  0.0 116.4 jit_solution(14522565491954827259)
XLA Ops:
  0.9 0.8 convert_bitcast_fusion
  1.7 0.7 fusion.81
  2.3 0.2 convert_reduce_fusion.2
  2.5 0.7 convert_reduce_fusion
  3.2 0.1 convolution_convert_fusion.4
  3.6 1.0 convolution_convert_fusion.3
  4.6 13.3 %to_owners.1 = (bf16[2,16,16,128]{3,2,1,0:T(8,128)(2,1)S(1)}, s32[16,1,128]{2,1,0:T(1,128)S(1)}) custom-call(bf16[16,16,128]{2,1,0:T(8,128)(2,1)S(1)} %reshape.360.src, s32[16,1,128]{2,1,0:T(1,128)S(1)} %reshape.361.src_notes), custom_call_target="tpu_custom_call" | custom-call | tf_op jit(solution)/shard_map/to_owners/pallas_call | solution.py:377
  17.9 0.5 broadcast.489
  18.4 0.7 reduce.9
  19.2 0.2 convert_reduce_fusion.1
  19.3 0.2 fusion.66
  19.6 0.2 select_reduce_fusion.1
  19.9 0.2 convert_reduce_fusion.3
  20.2 0.4 select_reduce_fusion
  20.7 0.1 multiply_cosine_fusion.1
  20.8 0.1 fusion.10.order_ref
  21.1 0.1 fusion.4
  21.2 0.8 fusion.6
  22.1 0.5 fusion.24.refs_1_
  22.5 4.0 %convolution_convert_fusion.1 = bf16[32,1536]{1,0:T(8,128)(2,1)S(1)} fusion(bf16[32,2048]{1,0:T(8,128)(2,1)S(1)} %fusion.6, bf16[2048,1536]{1,0:T(8,128)(2,1)} %param.19), kind=kOutput, calls=%fused_computation.1 | convolution fusion | flops 201375744 | bytes 6520832 | tf_op jit(solution)/shard_map/dot_general | solution.py:915
  26.5 0.2 reshape.366
  26.7 0.1 subtract_convert_fusion
  26.9 0.3 fusion.22
  27.1 0.2 copy.62
  27.3 0.1 pad_maximum_fusion.1.refs_0_
  27.4 11.3 %swap_pair_1.1 = (bf16[32,8,576]{2,1,0:T(8,128)(2,1)S(1)}, f32[32,576]{1,0:T(8,128)S(1)}) custom-call(bf16[32,8,576]{2,1,0:T(8,128)(2,1)S(1)} %pad_maximum_fusion.1.refs_0_, f32[32,576]{1,0:T(8,128)S(1)} %fusion.24.refs_1_), custom_call_target="tpu_custom_call" | custom-call | tf_op jit(solution)/shard_map/swap_pair_1/pallas_call | solution.py:292
  38.7 0.1 pad_maximum_fusion.q_ref
  38.8 0.1 multiply_reduce_fusion
  38.9 0.1 fusion.38
  39.2 0.3 fusion.17
  39.5 6.5 %ragged_attend.1 = (f32[32,16,512]{2,1,0:T(8,128)S(1)}, f32[32,16,128]{2,1,0:T(8,128)S(1)}) custom-call(s32[60]{0:T(128)S(1)} %reshape.364.ids_ref, s32[64]{0:T(128)S(1)} %pad_add_fusion.bounds_ref, s32[1]{0:T(128)} %bitcast.4.base_ref, bf16[32,16,576]{2,1,0:T(8,128)(2,1)S(1)} %pad_maximum_fusion.q_ref, bf16[576,4992]{1,0:T(8,128)(2,1)} %bitcast.59), custom_call_target="tpu_custom_call" | custom-call | tf_op jit(solution)/shard_map/ragged_attend/pallas_call | solution.py:824
  46.0 0.1 reduce_sum.77
  46.2 0.1 reshape.368.refs_1_
  46.4 7.3 %swap_pair_2.1 = (bf16[256,512]{1,0:T(8,128)(2,1)S(1)}, f32[2,128]{1,0:T(2,128)S(1)}) custom-call(bf16[256,512]{1,0:T(8,128)(2,1)S(1)} %fusion.8.refs_0_, f32[2,128]{1,0:T(2,128)S(1)} %reshape.368.refs_1_), custom_call_target="tpu_custom_call" | custom-call | tf_op jit(solution)/shard_map/swap_pair_2/pallas_call | solution.py:292
  53.8 0.2 fusion.3
  54.0 1.5 %fusion = bf16[8,4,8,128]{3,2,1,0:T(8,128)(2,1)S(1)} fusion(bf16[8,512,128]{2,1,0:T(8,128)(2,1)} %param.22, bf16[32,8,512]{2,1,0:T(8,128)(2,1)S(1)} %fusion.3), kind=kOutput, calls=%fused_computation.4 | convolution fusion | flops 33587200 | bytes 1376256 | tf_op jit(solution)/shard_map/bhl,hld->bhd/dot_general | solution.py:973
  55.5 3.0 %fusion.19 = f32[32,2048]{1,0:T(8,128)S(1)} fusion(bf16[1024,2048]{1,0:T(8,128)(2,1)} %param.23, bf16[8,4,8,128]{3,2,1,0:T(8,128)(2,1)S(1)} %fusion), kind=kOutput, calls=%fused_computation.42 | convolution fusion | flops 134217728 | bytes 4521984 | tf_op jit(solution)/shard_map/dot_general | solution.py:975
  58.6 5.0 %swap_pair_3.1 = f32[32,1024]{1,0:T(8,128)S(1)} custom-call(f32[32,1024]{1,0:T(8,128)S(1)} %constant_dynamic-slice_fusion.refs_0_), custom_call_target="tpu_custom_call" | custom-call | tf_op jit(solution)/shard_map/swap_pair_3/pallas_call | solution.py:292
  63.6 0.1 fusion.15
  63.8 0.1 concatenate.52
  64.0 0.1 fusion.93
  64.1 0.1 subtract_convert_fusion.1
  64.5 1.8 %copy-done.1 = bf16[1,2048,704]{1,2,0:T(8,128)(2,1)S(1)} copy-done((bf16[1,2048,704]{1,2,0:T(8,128)(2,1)S(1)}, bf16[1,2048,704]{1,2,0:T(8,128)(2,1)}, u32[]{:S(2)}) %copy-start.1) | copy-done | bytes 2883608
  66.3 22.7 %gather_experts.1 = bf16[2,16,16,2048]{3,2,1,0:T(8,128)(2,1)S(1)} custom-call(bf16[32,1152]{1,0:T(8,128)(2,1)S(1)} %pad_maximum_fusion.3.src, bf16[704,2048]{1,0:T(8,128)(2,1)S(1)} %bitcast.57, bf16[704,2048]{1,0:T(8,128)(2,1)} %bitcast.60, bf16[704,2048]{1,0:T(8,128)(2,1)} %bitcast.61, bf16[256,256]{1,0:T(8,128)(2,1)S(1)} %fusion.10.order_ref, ...), custom_call_target="tpu_custom_call" | custom-call | tf_op jit(solution)/shard_map/gather_experts/pallas_call | solution.py:548
  89.0 25.8 %scatter_sums.1 = (bf16[2,16,1024]{2,1,0:T(8,128)(2,1)S(1)}, bf16[16,32,128]{2,1,0:T(8,128)(2,1)S(1)}) custom-call(bf16[2,2,2,4,16,2048]{5,4,3,2,1,0:T(8,128)(2,1)S(1)} %bitcast.56, bf16[16,32,128]{2,1,0:T(8,128)(2,1)S(1)} %reshape.372.back_src), custom_call_target="tpu_custom_call" | custom-call | tf_op jit(solution)/shard_map/scatter_sums/pallas_call | solution.py:742
  114.9 0.2 convolution_convert_fusion
  115.1 0.6 slice.110
  115.7 0.7 fusion.90
  (57 shorter events, 1.9 us)
Async XLA Ops:
  0.6 21.4 %copy-start = (bf16[1024,576]{0,1:T(8,128)(2,1)S(1)}, bf16[1024,576]{0,1:T(8,128)(2,1)}, u32[]{:S(2)}) copy-start(bf16[1024,576]{0,1:T(8,128)(2,1)} %param.20) | copy-start | bytes 3538948
  22.5 4.4 %copy-start.2 = (bf16[8,128,512]{2,1,0:T(8,128)(2,1)S(1)}, bf16[8,128,512]{2,1,0:T(8,128)(2,1)}, u32[]{:S(2)}) copy-start(bf16[8,128,512]{2,1,0:T(8,128)(2,1)} %param.21) | copy-start | bytes 3145732
  55.5 8.4 %copy-start.4 = (f32[1024]{0:T(1024)S(1)}, f32[1024]{0:T(1024)}, u32[]{:S(2)}) copy-start(f32[1024]{0:T(1024)} %param.27) | copy-start | bytes 12292
  55.5 8.4 %copy-start.3 = (bf16[1024,16]{0,1:T(8,128)(2,1)S(1)}, bf16[1024,16]{0,1:T(8,128)(2,1)}, u32[]{:S(2)}) copy-start(bf16[1024,16]{0,1:T(8,128)(2,1)} %param.28) | copy-start | bytes 98308
  64.5 1.8 %copy-start.1 = (bf16[1,2048,704]{1,2,0:T(8,128)(2,1)S(1)}, bf16[1,2048,704]{1,2,0:T(8,128)(2,1)}, u32[]{:S(2)}) copy-start(bf16[1,2048,704]{1,2,0:T(8,128)(2,1)} %param.30) | copy-start | bytes 8650756

commit v4 on v3

--- a/solution.py
+++ b/solution.py
@@ -396,7 +396,7 @@
     )(blocks, notes)
 
 
-def gather_experts(block, gate, up, down, order, select, peers, number):
+def route_and_sum(block, gate, up, down, order, select, back, peers, number):
     rows, width = block.shape
     half = rows // 2
     layers = peers // 4
@@ -405,8 +405,10 @@
     some = rows * peers // 2
 
     def kernel(
-        src, gate_any, up_any, down_any, order_ref, select_ref, terms, out,
-        gate_ref, up_ref, down_ref, send_sem, recv_sem, own_sem, weight_sem,
+        src, gate_any, up_any, down_any, order_ref, select_ref, back_src, result, back_out,
+        out, gate_ref, up_ref, down_ref, terms, got_core, kept, got_first, mid, got_second,
+        last, got_z, send_sem, recv_sem, own_sem, weight_sem, sum_sends, sum_recvs,
+        back_sends, back_recvs,
     ):
         tok, x = lax.axis_index("tok"), lax.axis_index("head")
         z, y, core = tok // 4, (tok // 2) % 2, tok % 2
@@ -418,7 +420,8 @@
         across_y = (place(z, 1 - y, core), x)
         sibling = (place(z, y, 1 - core), x)
         along_z = [(place(lax.rem(z + d, layers), y, core), x) for d in range(1, layers)]
-        meet([across_x, across_y, sibling] + along_z)
+        others = [lax.rem(tok + d, peers) for d in range(1, peers)]
+        meet([across_x] + [(there, x) for there in others])
 
         def spot(z_, y_, core_, x_, h):
             start = place(z_, y_, core_) * rows + (h or 0) * half
@@ -462,7 +465,7 @@
             push(along_z[d - 1], z, y, core, x, None, True)
         for target in (across_x, across_y, sibling):
             push(target, z, y, core, x, None, True)
-        own = pltpu.make_async_copy(src, spot(z, y, core, x, None), own_sem)
+        own = pltpu.make_async_copy(src, spot(z, y, core, x, None), own_sem.at[0])
         own.start()
         weights = [
             pltpu.make_async_copy(a, b, weight_sem.at[i])
@@ -499,6 +502,21 @@
         for z_ in pairs[1]:
             second(z_)
 
+        backs = []
+        for i, there in enumerate(others):
+            copy = pltpu.make_async_remote_copy(
+                src_ref=back_src.at[there],
+                dst_ref=back_out.at[tok],
+                send_sem=back_sends.at[i],
+                recv_sem=back_recvs.at[tok],
+                device_id=(there, x),
+                device_id_type=MESH_ID,
+            )
+            copy.start()
+            backs.append(copy)
+        own_back = pltpu.make_async_copy(back_src.at[tok], back_out.at[tok], own_sem.at[1])
+        own_back.start()
+
         def across(a, b):
             return lax.dot_general(
                 a, b, (((1,), (1,)), ((), ())), preferred_element_type=jnp.float32
@@ -507,7 +525,7 @@
         def product(a, b):
             return jnp.dot(a, b, preferred_element_type=jnp.float32)
 
-        def expert(group):
+        def expert(a, group):
             at = pl.ds(pl.multiple_of(group * some, some), some)
             left, right = out[at, part:width], out[at, width + part :]
             logits = product(left, select_ref[:, :128]) + product(right, select_ref[:, :128])
@@ -528,150 +546,103 @@
             moved = product(order_ref[...], activity.astype(out.dtype)).astype(out.dtype)
             for k in range(0, full, 512):
                 piece = product(moved, down_ref[:, k : k + 512]).astype(terms.dtype)
-                terms[group, :, :, k : k + 512] = piece.reshape(peers, half, 512)
-
-        for g, pair in enumerate(pairs):
+                terms[a, :, :, k : k + 512] = piece.reshape(peers, half, 512)
+
+        def copy_to(target, source, dest, index, landing=None):
+            copy = pltpu.make_async_remote_copy(
+                src_ref=source,
+                dst_ref=dest,
+                send_sem=sum_sends.at[index],
+                recv_sem=sum_recvs.at[index if landing is None else landing],
+                device_id=target,
+                device_id_type=MESH_ID,
+            )
+            copy.start()
+            return copy
+
+        def columns(x_):
+            return pl.ds(pl.multiple_of(x_ * part, 128), part)
+
+        def total(first, second):
+            return first.astype(jnp.float32) + second.astype(jnp.float32)
+
+        def hand_over(a):
+            return [
+                copy_to(
+                    sibling,
+                    terms.at[a, pl.ds(((1 - core) * 2 + y_) * layers, layers)],
+                    got_core.at[a, y_],
+                    2 * a + g,
+                )
+                for g, y_ in enumerate((1 - y, y))
+            ]
+
+        def fold_core(a, y_):
+            @pl.loop(0, layers)
+            def _(z_):
+                kept[a, y_, z_] = total(
+                    terms[a, (core * 2 + y_) * layers + z_], got_core[a, y_, z_]
+                ).astype(kept.dtype)
+
+        def bring(pair):
             for z_ in pair:
                 third(z_)
             for z_ in pair:
                 for y_ in (y, 1 - y):
                     for x_ in (x, 1 - x):
                         land(z_, y_, 1 - core, x_, None)
-            if g == 0:
-                own.wait()
-                for copy in weights:
-                    copy.wait()
-            expert(pair[0] // 2)
-        for copy in sends:
-            copy.wait_send()
-
-    return pl.pallas_call(
-        kernel,
-        out_shape=jax.ShapeDtypeStruct((2, peers, half, full), block.dtype),
-        in_specs=in_vmem(1) + [pl.BlockSpec(memory_space=pl.ANY)] * 3 + in_vmem(2),
-        out_specs=in_vmem(1)[0],
-        scratch_shapes=[
-            pltpu.VMEM((rows * peers, 2 * width), block.dtype),
-            pltpu.VMEM((units, full), block.dtype),
-            pltpu.VMEM((units, full), block.dtype),
-            pltpu.VMEM((units, full), block.dtype),
-            pltpu.SemaphoreType.DMA((64,)),
-            pltpu.SemaphoreType.DMA((4 * peers,)),
-            pltpu.SemaphoreType.DMA,
-            pltpu.SemaphoreType.DMA((3,)),
-        ],
-        compiler_params=pltpu.CompilerParams(
-            collective_id=number, has_side_effects=True, vmem_limit_bytes=VMEM_LIMIT
-        ),
-        name="gather_experts",
-    )(block, gate, up, down, order, select)
-
-
-def scatter_sums(parts, back, peers, number):
-    layers = parts.shape[3]
-    half, full = parts.shape[4:]
-    width = full // 2
-
-    def kernel(
-        src, back_src, out, back_out, got_core, kept, got_first, mid, got_second, last, got_z,
-        sends, recvs, back_sends, back_recvs, own_sem,
-    ):
-        tok, x = lax.axis_index("tok"), lax.axis_index("head")
-        z, y, core = tok // 4, (tok // 2) % 2, tok % 2
-
-        def place(z_, y_, core_):
-            return z_ * 4 + y_ * 2 + core_
-
-        across_x = (tok, 1 - x)
-        across_y = (place(z, 1 - y, core), x)
-        sibling = (place(z, y, 1 - core), x)
-        along_z = [(place(lax.rem(z + d, layers), y, core), x) for d in range(1, layers)]
-        others = [lax.rem(tok + d, peers) for d in range(1, peers)]
-        meet([across_x] + [(there, x) for there in others])
-
-        def copy_to(target, source, dest, index):
-            copy = pltpu.make_async_remote_copy(
-                src_ref=source,
-                dst_ref=dest,
-                send_sem=sends.at[index],
-                recv_sem=recvs.at[index],
-                device_id=target,
-                device_id_type=MESH_ID,
-            )
-            copy.start()
-            return copy
-
-        def columns(x_):
-            return pl.ds(pl.multiple_of(x_ * width, 128), width)
-
-        def total(first, second):
-            return first.astype(jnp.float32) + second.astype(jnp.float32)
-
-        cores = [[None, None], [None, None]]
-        for g in range(2):
-            for h in range(2):
-                y_ = (1 - y) if g == 0 else y
-                cores[h][g] = copy_to(
-                    sibling, src.at[h, 1 - core, y_], got_core.at[h, y_], 2 * h + g
+
+        bring(pairs[0])
+        own.wait()
+        for copy in weights:
+            copy.wait()
+        expert(0, z // 2)
+        cores = [hand_over(0)]
+        bring(pairs[1])
+        first_x = []
+        for g, y_ in enumerate((1 - y, y)):
+            cores[0][g].wait_recv()
+            fold_core(0, y_)
+            first_x.append(
+                copy_to(
+                    across_x,
+                    kept.at[0, y_, slice(None), slice(None), columns(1 - x)],
+                    got_first.at[0, slice(None), slice(None), pl.ds(g * part, part)],
+                    5 + g,
                 )
-
-        backs = []
-        for i, there in enumerate(others):
-            copy = pltpu.make_async_remote_copy(
-                src_ref=back_src.at[there],
-                dst_ref=back_out.at[tok],
-                send_sem=back_sends.at[i],
-                recv_sem=back_recvs.at[tok],
-                device_id=(there, x),
-                device_id_type=MESH_ID,
-            )
-            copy.start()
-            backs.append(copy)
-        own = pltpu.make_async_copy(back_src.at[tok], back_out.at[tok], own_sem)
-        own.start()
-
-        def fold_core(h, y_):
-            @pl.loop(0, layers)
-            def _(z_):
-                kept[h, y_, z_] = total(src[h, core, y_, z_], got_core[h, y_, z_]).astype(
-                    kept.dtype
-                )
-
+            )
+        expert(1, 1 - z // 2)
+        cores.append(hand_over(1))
         cores[1][0].wait_recv()
         fold_core(1, 1 - y)
         first_y = copy_to(across_y, kept.at[1, 1 - y], got_first.at[1], 4)
-        cores[0][0].wait_recv()
-        fold_core(0, 1 - y)
-        first_x = [
-            copy_to(
-                across_x,
-                kept.at[0, 1 - y, slice(None), slice(None), columns(1 - x)],
-                got_first.at[0, slice(None), slice(None), pl.ds(0, width)],
-                5,
-            )
-        ]
-        cores[0][1].wait_recv()
-        fold_core(0, y)
-        first_x.append(
-            copy_to(
-                across_x,
-                kept.at[0, y, slice(None), slice(None), columns(1 - x)],
-                got_first.at[0, slice(None), slice(None), pl.ds(width, width)],
-                6,
-            )
-        )
-        cores[1][1].wait_recv()
-        fold_core(1, y)
-
         first_x[0].wait_recv()
 
         @pl.loop(0, layers)
         def _(z_):
             mid[0, z_] = total(
-                kept[0, 1 - y, z_, :, columns(x)], got_first[0, z_, :, :width]
+                kept[0, 1 - y, z_, :, columns(x)], got_first[0, z_, :, :part]
             ).astype(mid.dtype)
 
         second_y = copy_to(across_y, mid.at[0], got_second.at[0], 7)
+        cores[1][1].wait_recv()
+        fold_core(1, y)
+        first_x[1].wait_recv()
+        zs = []
+
+        def send_z(a):
+            group = (z // 2) if a == 0 else (1 - z // 2)
+            for d in range(1, layers):
+                z_ = lax.rem(z + d, layers)
+                zs.append(
+                    copy_to(
+                        along_z[d - 1],
+                        last.at[a, z_],
+                        got_z.at[group, d - 1],
+                        9 + a * layers + d - 1,
+                        9 + group * layers + d - 1,
+                    )
+                )
 
         first_y.wait_recv()
 
@@ -682,25 +653,12 @@
             ).astype(mid.dtype)
 
         second_x = copy_to(across_x, mid.at[1], got_second.at[1], 8)
-        first_x[1].wait_recv()
-
-        zs = []
-
-        def send_z(h):
-            for d in range(1, layers):
-                z_ = lax.rem(z + d, layers)
-                zs.append(
-                    copy_to(
-                        along_z[d - 1], last.at[h, z_], got_z.at[h, d - 1], 9 + h * layers + d - 1
-                    )
-                )
-
         second_y.wait_recv()
 
         @pl.loop(0, layers)
         def _(z_):
             last[0, z_] = (
-                total(kept[0, y, z_, :, columns(x)], got_first[0, z_, :, width:])
+                total(kept[0, y, z_, :, columns(x)], got_first[0, z_, :, part:])
                 + got_second[0, z_].astype(jnp.float32)
             ).astype(last.dtype)
 
@@ -717,55 +675,64 @@
         send_z(1)
         for copy in zs:
             copy.wait_recv()
-        for h in range(2):
-            acc = last[h, z].astype(jnp.float32)
+        for a in range(2):
+            group = (z // 2) if a == 0 else (1 - z // 2)
+            acc = last[a, z].astype(jnp.float32)
             for d in range(1, layers):
-                acc = acc + got_z[h, d - 1].astype(jnp.float32)
-            out[h] = acc.astype(out.dtype)
+                acc = acc + got_z[group, d - 1].astype(jnp.float32)
+            result[group] = acc.astype(result.dtype)
         for there in others:
-            spot = back_out.at[there]
+            spot_back = back_out.at[there]
             pltpu.make_async_remote_copy(
-                src_ref=spot,
-                dst_ref=spot,
+                src_ref=spot_back,
+                dst_ref=spot_back,
                 send_sem=back_sends.at[0],
                 recv_sem=back_recvs.at[there],
                 device_id=sibling,
                 device_id_type=MESH_ID,
             ).wait_recv()
-        for copy in backs:
+        own_back.wait()
+        for copy in (
+            sends + backs + cores[0] + cores[1] + first_x + [first_y, second_y, second_x] + zs
+        ):
             copy.wait_send()
-        own.wait()
-        for copy in cores[0] + cores[1] + first_x + [first_y, second_y, second_x] + zs:
-            copy.wait_send()
-
-    kind = parts.dtype
+
+    kind = block.dtype
     return pl.pallas_call(
         kernel,
         out_shape=[
-            jax.ShapeDtypeStruct((2, half, width), kind),
-            jax.ShapeDtypeStruct(back.shape, back.dtype),
+            jax.ShapeDtypeStruct((2, half, part), kind),
+            jax.ShapeDtypeStruct(back.shape, kind),
         ],
-        in_specs=in_vmem(2),
+        in_specs=in_vmem(1) + [pl.BlockSpec(memory_space=pl.ANY)] * 3 + in_vmem(3),
         out_specs=in_vmem(2),
         scratch_shapes=[
+            pltpu.VMEM((rows * peers, 2 * width), block.dtype),
+            pltpu.VMEM((units, full), block.dtype),
+            pltpu.VMEM((units, full), block.dtype),
+            pltpu.VMEM((units, full), block.dtype),
+            pltpu.VMEM((2, peers, half, full), kind),
             pltpu.VMEM((2, 2, layers, half, full), kind),
             pltpu.VMEM((2, 2, layers, half, full), kind),
             pltpu.VMEM((2, layers, half, full), kind),
-            pltpu.VMEM((2, layers, half, width), kind),
-            pltpu.VMEM((2, layers, half, width), kind),
-            pltpu.VMEM((2, layers, half, width), kind),
-            pltpu.VMEM((2, layers - 1, half, width), kind),
+            pltpu.VMEM((2, layers, half, part), kind),
+            pltpu.VMEM((2, layers, half, part), kind),
+            pltpu.VMEM((2, layers, half, part), kind),
+            pltpu.VMEM((2, layers - 1, half, part), kind),
+            pltpu.SemaphoreType.DMA((64,)),
+            pltpu.SemaphoreType.DMA((4 * peers,)),
+            pltpu.SemaphoreType.DMA((2,)),
+            pltpu.SemaphoreType.DMA((3,)),
             pltpu.SemaphoreType.DMA((9 + 2 * layers,)),
             pltpu.SemaphoreType.DMA((9 + 2 * layers,)),
             pltpu.SemaphoreType.DMA((peers,)),
             pltpu.SemaphoreType.DMA((peers,)),
-            pltpu.SemaphoreType.DMA,
         ],
         compiler_params=pltpu.CompilerParams(
             collective_id=number, has_side_effects=True, vmem_limit_bytes=VMEM_LIMIT
         ),
-        name="scatter_sums",
-    )(parts, back)
+        name="route_and_sum",
+    )(block, gate, up, down, order, select, back)
 
 
 def ragged_attend(queries, cache, ids, bounds, base, factor):
@@ -1010,19 +977,19 @@
         ],
         axis=1,
     ).astype(bf16)
-    terms = gather_experts(
+    back = jnp.concatenate([attended, new_entry], axis=1)
+    back = jnp.pad(back, ((0, 0), (0, 2 * part - back.shape[1])))
+    summed, back = route_and_sum(
         jnp.concatenate([gained, notes], axis=1),
         expert_gate[0].T,
         expert_up[0].T,
         expert_down[0],
         order,
         select,
+        back.reshape(peers, each * 2 * part // 128, 128),
         peers,
         4,
-    ).reshape(2, 2, 2, layers, half, 2 * part)
-    back = jnp.concatenate([attended, new_entry], axis=1)
-    back = jnp.pad(back, ((0, 0), (0, 2 * part - back.shape[1])))
-    summed, back = scatter_sums(terms, back.reshape(peers, each * 2 * part // 128, 128), peers, 5)
+    )
     mixed_back = jnp.concatenate([back.reshape(rows, 2 * part), summed.reshape(rows, part)], axis=1)
     final = pick_rows(placed.T, mixed_back)
     return (

time: 117 us -> 116 us (level)
    pallas_call x2 -> x1, Pallas kernels: 48.5 us -> 48.1 us  [route_and_sum(): pl.pallas_call(kernel, out_shape=[jax.ShapeDtypeStruct((2, half, part), k...]
where the time goes in v4:
time: 116 us
  Pallas kernels  91.4 us (79%)
  matrix products  11 us (9%)
  other arithmetic  7.27 us (6%)
  local copies, waits for them, and re-layouts  5.16 us (4%)
    pallas_call x1, Pallas kernels, route_and_sum(): pl.pallas_call(kernel, out_shape=[jax.ShapeDtypeStruct((2, half, part), k...  48.1 us
    pallas_call x3, Pallas kernels, swap_pair(): pl.pallas_call(kernel, out_shape=[jax.ShapeDtypeStruct(a.shape, a.dtype)...  23.6 us
    pallas_call x1, Pallas kernels, to_owners(): pl.pallas_call(kernel, out_shape=[jax.ShapeDtypeStruct((2,) + blocks.shap...  13.3 us
    pallas_call x1, Pallas kernels, ragged_attend(): pl.pallas_call(kernel, out_shape=[jax.ShapeDtypeStruct((slots, heads, LAT...  6.48 us
    dot_general x1, matrix products, direct_body(): queries = jnp.dot(normed, w_query, preferred_element_type=f32).astype(bf16)  4.01 us
    dot_general x1, matrix products, direct_body(): piece = jnp.dot(head_out, w_out, preferred_element_type=f32)  3.02 us

profile of v4, /device:TPU:0, one launch (start us, length us, event | category | flops | bytes accessed | tf_op | source)
XLA Modules:
  0.0 116.0 jit_solution(7051365898166606122)
XLA Ops:
  0.6 0.8 fusion.81
  1.4 0.2 convert_reduce_fusion.2
  1.6 0.7 convert_bitcast_fusion
  2.3 0.7 convert_reduce_fusion
  3.0 0.1 convolution_convert_fusion.4
  3.2 1.0 convolution_convert_fusion.3
  4.2 13.3 %to_owners.1 = (bf16[2,16,16,128]{3,2,1,0:T(8,128)(2,1)S(1)}, s32[16,1,128]{2,1,0:T(1,128)S(1)}) custom-call(bf16[16,16,128]{2,1,0:T(8,128)(2,1)S(1)} %reshape.357.src, s32[16,1,128]{2,1,0:T(1,128)S(1)} %reshape.358.src_notes), custom_call_target="tpu_custom_call" | custom-call | tf_op jit(solution)/shard_map/to_owners/pallas_call | solution.py:377
  17.6 0.1 fusion.4
  17.7 0.8 fusion.6
  18.6 4.0 %convolution_convert_fusion.1 = bf16[32,1536]{1,0:T(8,128)(2,1)S(1)} fusion(bf16[32,2048]{1,0:T(8,128)(2,1)S(1)} %fusion.6, bf16[2048,1536]{1,0:T(8,128)(2,1)} %param.19), kind=kOutput, calls=%fused_computation.1 | convolution fusion | flops 201375744 | bytes 6520832 | tf_op jit(solution)/shard_map/dot_general | solution.py:882
  22.6 0.2 reshape.363
  22.8 0.5 broadcast.489
  23.3 0.7 reduce.9
  24.0 0.2 fusion.66
  24.2 0.2 select_reduce_fusion.1
  24.4 0.1 multiply_cosine_fusion.1
  24.6 0.1 subtract_convert_fusion
  24.7 0.3 fusion.22
  25.0 0.2 copy.62
  25.1 0.1 pad_maximum_fusion.1.refs_0_
  25.2 0.4 fusion.24.refs_1_
  25.7 11.3 %swap_pair_1.1 = (bf16[32,8,576]{2,1,0:T(8,128)(2,1)S(1)}, f32[32,576]{1,0:T(8,128)S(1)}) custom-call(bf16[32,8,576]{2,1,0:T(8,128)(2,1)S(1)} %pad_maximum_fusion.1.refs_0_, f32[32,576]{1,0:T(8,128)S(1)} %fusion.24.refs_1_), custom_call_target="tpu_custom_call" | custom-call | tf_op jit(solution)/shard_map/swap_pair_1/pallas_call | solution.py:292
  37.0 0.1 multiply_reduce_fusion
  37.2 0.2 convert_reduce_fusion.1
  37.4 0.1 fusion.38
  37.6 0.3 fusion.17
  37.9 0.1 pad_maximum_fusion.q_ref
  38.3 0.2 convert_reduce_fusion.3
  38.5 0.4 select_reduce_fusion
  39.0 0.1 reshape.361.ids_ref
  39.1 6.5 %ragged_attend.1 = (f32[32,16,512]{2,1,0:T(8,128)S(1)}, f32[32,16,128]{2,1,0:T(8,128)S(1)}) custom-call(s32[60]{0:T(128)S(1)} %reshape.361.ids_ref, s32[64]{0:T(128)S(1)} %pad_add_fusion.bounds_ref, s32[1]{0:T(128)} %bitcast.4.base_ref, bf16[32,16,576]{2,1,0:T(8,128)(2,1)S(1)} %pad_maximum_fusion.q_ref, bf16[576,4992]{1,0:T(8,128)(2,1)} %bitcast.57), custom_call_target="tpu_custom_call" | custom-call | tf_op jit(solution)/shard_map/ragged_attend/pallas_call | solution.py:791
  45.6 0.1 reduce_sum.77
  45.8 0.1 reshape.365.refs_1_
  45.9 7.3 %swap_pair_2.1 = (bf16[256,512]{1,0:T(8,128)(2,1)S(1)}, f32[2,128]{1,0:T(2,128)S(1)}) custom-call(bf16[256,512]{1,0:T(8,128)(2,1)S(1)} %fusion.8.refs_0_, f32[2,128]{1,0:T(2,128)S(1)} %reshape.365.refs_1_), custom_call_target="tpu_custom_call" | custom-call | tf_op jit(solution)/shard_map/swap_pair_2/pallas_call | solution.py:292
  53.3 0.2 fusion.3
  53.5 1.5 %fusion = bf16[8,4,8,128]{3,2,1,0:T(8,128)(2,1)S(1)} fusion(bf16[8,512,128]{2,1,0:T(8,128)(2,1)} %param.22, bf16[32,8,512]{2,1,0:T(8,128)(2,1)S(1)} %fusion.3), kind=kOutput, calls=%fused_computation.4 | convolution fusion | flops 33587200 | bytes 1376256 | tf_op jit(solution)/shard_map/bhl,hld->bhd/dot_general | solution.py:940
  55.0 3.0 %fusion.19 = f32[32,2048]{1,0:T(8,128)S(1)} fusion(bf16[1024,2048]{1,0:T(8,128)(2,1)} %param.23, bf16[8,4,8,128]{3,2,1,0:T(8,128)(2,1)S(1)} %fusion), kind=kOutput, calls=%fused_computation.42 | convolution fusion | flops 134217728 | bytes 4521984 | tf_op jit(solution)/shard_map/dot_general | solution.py:942
  58.1 5.0 %swap_pair_3.1 = f32[32,1024]{1,0:T(8,128)S(1)} custom-call(f32[32,1024]{1,0:T(8,128)S(1)} %constant_dynamic-slice_fusion.refs_0_), custom_call_target="tpu_custom_call" | custom-call | tf_op jit(solution)/shard_map/swap_pair_3/pallas_call | solution.py:292
  63.2 0.1 fusion.15
  63.3 0.1 concatenate.52
  63.6 0.1 fusion.93
  63.8 0.1 fusion.65
  64.3 0.1 fusion.10.order_ref
  64.5 1.8 %copy-done.1 = bf16[1,2048,704]{1,2,0:T(8,128)(2,1)S(1)} copy-done((bf16[1,2048,704]{1,2,0:T(8,128)(2,1)S(1)}, bf16[1,2048,704]{1,2,0:T(8,128)(2,1)}, u32[]{:S(2)}) %copy-start.1) | copy-done | bytes 2883608
  66.3 48.1 %route_and_sum.1 = (bf16[2,16,1024]{2,1,0:T(8,128)(2,1)S(1)}, bf16[16,32,128]{2,1,0:T(8,128)(2,1)S(1)}) custom-call(bf16[32,1152]{1,0:T(8,128)(2,1)S(1)} %pad_maximum_fusion.3.src, bf16[704,2048]{1,0:T(8,128)(2,1)S(1)} %bitcast.55, bf16[704,2048]{1,0:T(8,128)(2,1)} %bitcast.58, bf16[704,2048]{1,0:T(8,128)(2,1)} %bitcast.59, ...), custom_call_target="tpu_custom_call" | custom-call | tf_op jit(solution)/shard_map/route_and_sum/pallas_call | solution.py:701
  114.5 0.2 convolution_convert_fusion
  114.7 0.7 fusion.90
  115.4 0.6 slice.110
  (56 shorter events, 1.8 us)
Async XLA Ops:
  0.6 24.6 %copy-start = (bf16[1024,576]{0,1:T(8,128)(2,1)S(1)}, bf16[1024,576]{0,1:T(8,128)(2,1)}, u32[]{:S(2)}) copy-start(bf16[1024,576]{0,1:T(8,128)(2,1)} %param.20) | copy-start | bytes 3538948
  18.5 6.2 %copy-start.2 = (bf16[8,128,512]{2,1,0:T(8,128)(2,1)S(1)}, bf16[8,128,512]{2,1,0:T(8,128)(2,1)}, u32[]{:S(2)}) copy-start(bf16[8,128,512]{2,1,0:T(8,128)(2,1)} %param.21) | copy-start | bytes 3145732
  55.0 8.5 %copy-start.4 = (f32[1024]{0:T(1024)S(1)}, f32[1024]{0:T(1024)}, u32[]{:S(2)}) copy-start(f32[1024]{0:T(1024)} %param.27) | copy-start | bytes 12292
  55.0 8.5 %copy-start.3 = (bf16[1024,16]{0,1:T(8,128)(2,1)S(1)}, bf16[1024,16]{0,1:T(8,128)(2,1)}, u32[]{:S(2)}) copy-start(bf16[1024,16]{0,1:T(8,128)(2,1)} %param.28) | copy-start | bytes 98308
  64.5 1.8 %copy-start.1 = (bf16[1,2048,704]{1,2,0:T(8,128)(2,1)S(1)}, bf16[1,2048,704]{1,2,0:T(8,128)(2,1)}, u32[]{:S(2)}) copy-start(bf16[1,2048,704]{1,2,0:T(8,128)(2,1)} %param.30) | copy-start | bytes 8650756

commit v5 on v4

--- a/solution.py
+++ b/solution.py
@@ -253,6 +253,7 @@
 KEY_CUTS = (0, 384, 768, 1152, 1536, 1664)
 WINDOW = 4
 VMEM_LIMIT = 48 * 1024 * 1024
+ROUTE_VMEM_LIMIT = 60 * 1024 * 1024
 
 
 def meet(partners):
@@ -501,21 +502,6 @@
         second(near)
         for z_ in pairs[1]:
             second(z_)
-
-        backs = []
-        for i, there in enumerate(others):
-            copy = pltpu.make_async_remote_copy(
-                src_ref=back_src.at[there],
-                dst_ref=back_out.at[tok],
-                send_sem=back_sends.at[i],
-                recv_sem=back_recvs.at[tok],
-                device_id=(there, x),
-                device_id_type=MESH_ID,
-            )
-            copy.start()
-            backs.append(copy)
-        own_back = pltpu.make_async_copy(back_src.at[tok], back_out.at[tok], own_sem.at[1])
-        own_back.start()
 
         def across(a, b):
             return lax.dot_general(
@@ -613,6 +599,20 @@
             )
         expert(1, 1 - z // 2)
         cores.append(hand_over(1))
+        backs = []
+        for i, there in enumerate(others):
+            copy = pltpu.make_async_remote_copy(
+                src_ref=back_src.at[there],
+                dst_ref=back_out.at[tok],
+                send_sem=back_sends.at[i],
+                recv_sem=back_recvs.at[tok],
+                device_id=(there, x),
+                device_id_type=MESH_ID,
+            )
+            copy.start()
+            backs.append(copy)
+        own_back = pltpu.make_async_copy(back_src.at[tok], back_out.at[tok], own_sem.at[1])
+        own_back.start()
         cores[1][0].wait_recv()
         fold_core(1, 1 - y)
         first_y = copy_to(across_y, kept.at[1, 1 - y], got_first.at[1], 4)
@@ -729,7 +729,7 @@
             pltpu.SemaphoreType.DMA((peers,)),
         ],
         compiler_params=pltpu.CompilerParams(
-            collective_id=number, has_side_effects=True, vmem_limit_bytes=VMEM_LIMIT
+            collective_id=number, has_side_effects=True, vmem_limit_bytes=ROUTE_VMEM_LIMIT
         ),
         name="route_and_sum",
     )(block, gate, up, down, order, select, back)
@@ -990,12 +990,11 @@
         peers,
         4,
     )
-    mixed_back = jnp.concatenate([back.reshape(rows, 2 * part), summed.reshape(rows, part)], axis=1)
-    final = pick_rows(placed.T, mixed_back)
+    back = back.reshape(rows, 2 * part)
     return (
-        final[:, part : part + LATENT + ROPE],
-        final[:, :part],
-        final[:, 2 * part :],
+        pick_rows(placed.T, back[:, part : part + LATENT + ROPE]),
+        pick_rows(placed.T, back[:, :part]),
+        pick_rows(placed.T, summed.reshape(rows, part)),
     )
 
 

time: 116 us -> 121 us (1.043)
  matrix products: 11 us -> 14.1 us
  other arithmetic: 7.27 us -> 9.18 us
  local copies, waits for them, and re-layouts: 5.16 us -> 3.63 us
  Pallas kernels: 91.4 us -> 92.7 us
    dot_general x2 -> x4, matrix products: 1.23 us -> 4.32 us  [pick_rows(): jnp.dot(chosen.astype(jnp.bfloat16), values, preferred_element_type=jnp.f...]
    unnamed x10 -> x8, local copies, waits for them, and re-layouts: 1.84 us -> 0.03 us
    slice x2 -> x0, local copies, waits for them, and re-layouts: 1.28 us -> none  [the longest x1 0.66 us: direct_body(): final[:, 2 * part:]]
    pallas_call x1, Pallas kernels: 48.1 us -> 49.4 us  [route_and_sum(): pl.pallas_call(kernel, out_shape=[jax.ShapeDtypeStruct((2, half, part), k...]
where the time goes in v5:
time: 121 us
  Pallas kernels  92.7 us (77%)
  matrix products  14.1 us (12%)
  other arithmetic  9.18 us (8%)
  local copies, waits for them, and re-layouts  3.63 us (3%)
    pallas_call x1, Pallas kernels, route_and_sum(): pl.pallas_call(kernel, out_shape=[jax.ShapeDtypeStruct((2, half, part), k...  49.4 us
    pallas_call x3, Pallas kernels, swap_pair(): pl.pallas_call(kernel, out_shape=[jax.ShapeDtypeStruct(a.shape, a.dtype)...  23.6 us
    pallas_call x1, Pallas kernels, to_owners(): pl.pallas_call(kernel, out_shape=[jax.ShapeDtypeStruct((2,) + blocks.shap...  13.3 us
    pallas_call x1, Pallas kernels, ragged_attend(): pl.pallas_call(kernel, out_shape=[jax.ShapeDtypeStruct((slots, heads, LAT...  6.47 us
    dot_general x4, matrix products, pick_rows(): jnp.dot(chosen.astype(jnp.bfloat16), values, preferred_element_type=jnp.f...  4.32 us
    dot_general x1, matrix products, direct_body(): queries = jnp.dot(normed, w_query, preferred_element_type=f32).astype(bf16)  4.01 us
    dot_general x1, matrix products, direct_body(): piece = jnp.dot(head_out, w_out, preferred_element_type=f32)  3.02 us

profile of v5, /device:TPU:0, one launch (start us, length us, event | category | flops | bytes accessed | tf_op | source)
XLA Modules:
  0.0 120.6 jit_solution(18237706770965347665)
XLA Ops:
  0.6 0.8 fusion.82
  1.4 0.2 convert_reduce_fusion.2
  1.6 0.7 convert_bitcast_fusion
  2.3 0.7 convert_reduce_fusion
  3.0 0.1 convolution_convert_fusion.6
  3.2 1.0 convolution_convert_fusion.4
  4.2 13.3 %to_owners.1 = (bf16[2,16,16,128]{3,2,1,0:T(8,128)(2,1)S(1)}, s32[16,1,128]{2,1,0:T(1,128)S(1)}) custom-call(bf16[16,16,128]{2,1,0:T(8,128)(2,1)S(1)} %reshape.357.src, s32[16,1,128]{2,1,0:T(1,128)S(1)} %reshape.358.src_notes), custom_call_target="tpu_custom_call" | custom-call | tf_op jit(solution)/shard_map/to_owners/pallas_call | solution.py:378
  17.6 0.1 fusion.4
  17.7 0.8 fusion.6
  18.6 4.0 %convolution_convert_fusion = bf16[32,1536]{1,0:T(8,128)(2,1)S(1)} fusion(bf16[32,2048]{1,0:T(8,128)(2,1)S(1)} %fusion.6, bf16[2048,1536]{1,0:T(8,128)(2,1)} %param.19), kind=kOutput, calls=%fused_computation | convolution fusion | flops 201375744 | bytes 6520832 | tf_op jit(solution)/shard_map/dot_general | solution.py:882
  22.6 0.2 reshape.363
  22.8 0.5 broadcast.489
  23.3 0.7 reduce.9
  24.0 0.2 fusion.67
  24.2 0.2 select_reduce_fusion.1
  24.4 0.1 multiply_cosine_fusion.1
  24.6 0.1 subtract_convert_fusion
  24.7 0.3 fusion.20
  25.0 0.2 copy.62
  25.1 0.1 pad_maximum_fusion.1.refs_0_
  25.2 0.4 fusion.22.refs_1_
  25.7 11.3 %swap_pair_1.1 = (bf16[32,8,576]{2,1,0:T(8,128)(2,1)S(1)}, f32[32,576]{1,0:T(8,128)S(1)}) custom-call(bf16[32,8,576]{2,1,0:T(8,128)(2,1)S(1)} %pad_maximum_fusion.1.refs_0_, f32[32,576]{1,0:T(8,128)S(1)} %fusion.22.refs_1_), custom_call_target="tpu_custom_call" | custom-call | tf_op jit(solution)/shard_map/swap_pair_1/pallas_call | solution.py:293
  37.0 0.1 multiply_reduce_fusion
  37.2 0.2 convert_reduce_fusion.1
  37.4 0.1 fusion.37
  37.6 0.3 fusion.14
  37.9 0.1 pad_maximum_fusion.q_ref
  38.3 0.2 convert_reduce_fusion.3
  38.5 0.4 select_reduce_fusion
  39.1 6.5 %ragged_attend.1 = (f32[32,16,512]{2,1,0:T(8,128)S(1)}, f32[32,16,128]{2,1,0:T(8,128)S(1)}) custom-call(s32[60]{0:T(128)S(1)} %reshape.361.ids_ref, s32[64]{0:T(128)S(1)} %pad_add_fusion.bounds_ref, s32[1]{0:T(128)} %bitcast.4.base_ref, bf16[32,16,576]{2,1,0:T(8,128)(2,1)S(1)} %pad_maximum_fusion.q_ref, bf16[576,4992]{1,0:T(8,128)(2,1)} %bitcast.56), custom_call_target="tpu_custom_call" | custom-call | tf_op jit(solution)/shard_map/ragged_attend/pallas_call | solution.py:791
  45.6 0.1 reduce_sum.77
  45.9 7.3 %swap_pair_2.1 = (bf16[256,512]{1,0:T(8,128)(2,1)S(1)}, f32[2,128]{1,0:T(2,128)S(1)}) custom-call(bf16[256,512]{1,0:T(8,128)(2,1)S(1)} %fusion.8.refs_0_, f32[2,128]{1,0:T(2,128)S(1)} %reshape.365.refs_1_), custom_call_target="tpu_custom_call" | custom-call | tf_op jit(solution)/shard_map/swap_pair_2/pallas_call | solution.py:293
  53.3 0.2 fusion.3
  53.5 1.5 %fusion = bf16[8,4,8,128]{3,2,1,0:T(8,128)(2,1)S(1)} fusion(bf16[8,512,128]{2,1,0:T(8,128)(2,1)} %param.22, bf16[32,8,512]{2,1,0:T(8,128)(2,1)S(1)} %fusion.3), kind=kOutput, calls=%fused_computation.5 | convolution fusion | flops 33587200 | bytes 1376256 | tf_op jit(solution)/shard_map/bhl,hld->bhd/dot_general | solution.py:940
  55.0 3.0 %fusion.16 = f32[32,2048]{1,0:T(8,128)S(1)} fusion(bf16[1024,2048]{1,0:T(8,128)(2,1)} %param.23, bf16[8,4,8,128]{3,2,1,0:T(8,128)(2,1)S(1)} %fusion), kind=kOutput, calls=%fused_computation.41 | convolution fusion | flops 134217728 | bytes 4521984 | tf_op jit(solution)/shard_map/dot_general | solution.py:942
  58.1 5.0 %swap_pair_3.1 = f32[32,1024]{1,0:T(8,128)S(1)} custom-call(f32[32,1024]{1,0:T(8,128)S(1)} %constant_dynamic-slice_fusion.refs_0_), custom_call_target="tpu_custom_call" | custom-call | tf_op jit(solution)/shard_map/swap_pair_3/pallas_call | solution.py:293
  63.2 0.1 fusion.12
  63.3 0.1 concatenate.49
  63.4 0.7 reshape.368.back_src
  64.2 0.1 fusion.92
  64.7 0.6 pad_maximum_fusion.3.src
  65.5 0.7 add_convert_fusion.select_ref
  66.2 0.7 fusion.10.order_ref
  66.9 49.4 %route_and_sum.1 = (bf16[2,16,1024]{2,1,0:T(8,128)(2,1)}, bf16[16,32,128]{2,1,0:T(8,128)(2,1)}) custom-call(bf16[32,1152]{1,0:T(8,128)(2,1)} %pad_maximum_fusion.3.src, bf16[704,2048]{1,0:T(8,128)(2,1)} %bitcast.57, bf16[704,2048]{1,0:T(8,128)(2,1)} %bitcast.58, bf16[704,2048]{1,0:T(8,128)(2,1)} %bitcast.59, bf16[256,256]{1,0:T(8,128)(2,1)} %fusion.10.order_ref, ...), custom_call_target="tpu_custom_call" | custom-call | tf_op jit(solution)/shard_map/route_and_sum/pallas_call | solution.py:701
  116.3 1.0 reshape.369
  117.3 0.8 convolution_convert_fusion.3
  118.1 0.8 convolution_convert_fusion.5
  118.9 1.7 %convolution_convert_fusion.2 = bf16[32,1024]{1,0:T(8,128)(2,1)} fusion(bf16[32,1024]{1,0:T(8,128)(2,1)} %bitcast.62, s32[32]{0:T(128)S(1)} %multiply_add_fusion.1), kind=kOutput, calls=%fused_computation.2 | convolution fusion | flops 2130944 | bytes 131200 | tf_op jit(solution)/shard_map/dot_general | solution.py:815
  (54 shorter events, 1.9 us)
Async XLA Ops:
  0.6 24.6 %copy-start = (bf16[1024,576]{0,1:T(8,128)(2,1)S(1)}, bf16[1024,576]{0,1:T(8,128)(2,1)}, u32[]{:S(2)}) copy-start(bf16[1024,576]{0,1:T(8,128)(2,1)} %param.20) | copy-start | bytes 3538948
  18.5 6.2 %copy-start.1 = (bf16[8,128,512]{2,1,0:T(8,128)(2,1)S(1)}, bf16[8,128,512]{2,1,0:T(8,128)(2,1)}, u32[]{:S(2)}) copy-start(bf16[8,128,512]{2,1,0:T(8,128)(2,1)} %param.21) | copy-start | bytes 3145732
  55.0 9.1 %copy-start.3 = (f32[1024]{0:T(1024)S(1)}, f32[1024]{0:T(1024)}, u32[]{:S(2)}) copy-start(f32[1024]{0:T(1024)} %param.27) | copy-start | bytes 12292
  55.0 9.1 %copy-start.2 = (bf16[1024,16]{0,1:T(8,128)(2,1)S(1)}, bf16[1024,16]{0,1:T(8,128)(2,1)}, u32[]{:S(2)}) copy-start(bf16[1024,16]{0,1:T(8,128)(2,1)} %param.28) | copy-start | bytes 98308
